TPU v7x, 256 devices: a whole 4x4x8 slice. The times are simulated.
256 devices in a mesh: dp: 16 (over z, core), expert: 16 (over x, y).
Axes of the slice: x: 4, y: 4, z: 8, core: 2. Of those that a mesh axis runs over, the one named last changes fastest.
Arguments:
- tokens: bfloat16 [16, 1024, 4096], P('dp', 'expert'), may hold values from -6 to 6
- attn_gain: float32 [4096], replicated, may hold values from 0.1 to 1.9
- moe_gain: float32 [4096], replicated, may hold values from 0.1 to 1.9
- w_query: bfloat16 [4096, 4096], P('dp', 'expert'), may hold values from -4 to 4
- w_key: bfloat16 [4096, 256], P('dp'), may hold values from -0.1 to 0.1
- w_value: bfloat16 [4096, 256], P('dp'), may hold values from -0.09375 to 0.09375
- w_out: bfloat16 [4096, 4096], P('expert', 'dp'), may hold values from -0.09375 to 0.09375
- expert_gate: bfloat16 [16, 4096, 768], P('expert', 'dp'), may hold values from -0.09375 to 0.09375
- expert_up: bfloat16 [16, 4096, 768], P('expert', 'dp'), may hold values from -0.09375 to 0.09375
- expert_down: bfloat16 [16, 768, 4096], P('expert', 'dp'), may hold values from -0.21875 to 0.21875
- routes: int32 [16, 1024, 8], P('dp', 'expert'), may hold values from 0 to 15, all different within a row; in each aligned block of 64 rows (0 to 63, 64 to 127, ..., all dimensions but the last counted through in order) at most 48 rows name the same one
- route_weights: float32 [16, 1024, 8], P('dp', 'expert'), may hold values from 0.05 to 1
Outputs:
- layer_out: bfloat16 [16, 1024, 4096], P('dp', 'expert')
Inputs may be any that keep to these rules, and one draw needn't show every extreme that they name: `routes`: each token names 8 different experts; among the rows of one device no expert is named by more than 48 tokens, and in every draw some expert is named by exactly 48 tokens of some device.
All inputs are finite; a program needn't handle non-finite values.
Results may differ from a plain program's by a relative error of at most 0.012.
Values may be sent and summed in bfloat16 or wider, within the bound.
A program may use at most 128 MiB of HBM per device.

v0:
```python
import math

import jax
import jax.numpy as jnp
from jax import lax
from jax.sharding import PartitionSpec as P

HD = 128
EXPERTS = 16
CAP = 48


def rms_norm(values, gain):
    return values * lax.rsqrt(jnp.mean(values * values, axis=-1, keepdims=True) + 1e-06) * gain


def rotate(tensor, positions):
    half_dim = tensor.shape[-1] // 2
    frequency = jnp.exp(
        jnp.arange(half_dim, dtype=jnp.float32) * (-2.0 * math.log(1000000.0) / tensor.shape[-1])
    )
    angles = positions[:, None] * frequency[None, :]
    cosine = jnp.cos(angles)[:, None, :]
    sine_table = jnp.sin(angles)[:, None, :]
    lower_half = tensor[..., :half_dim]
    upper_half = tensor[..., half_dim:]
    return jnp.concatenate(
        [
            lower_half * cosine - upper_half * sine_table,
            upper_half * cosine + lower_half * sine_table,
        ],
        axis=-1,
    )


def add_rows(left_rows, pieces):
    return jnp.dot(left_rows, pieces, preferred_element_type=jnp.float32)


def run_experts(arrived, gate_shard, up_shard, down_shard):
    window_rows = arrived
    gate_sum = jnp.einsum(
        "ecd,edf->ecf",
        window_rows,
        lax.all_gather(gate_shard, "dp", axis=1, tiled=True),
        preferred_element_type=jnp.float32,
    )
    up_sum = jnp.einsum(
        "ecd,edf->ecf",
        window_rows,
        lax.all_gather(up_shard, "dp", axis=1, tiled=True),
        preferred_element_type=jnp.float32,
    )
    active = (jax.nn.silu(gate_sum) * up_sum).astype(jnp.bfloat16)
    window_rows = active
    produced = jnp.einsum(
        "ecf,efd->ecd",
        window_rows,
        lax.all_gather(down_shard, "dp", axis=1, tiled=True),
        preferred_element_type=jnp.float32,
    )
    return produced.astype(jnp.bfloat16)


def share_table(picked_ids, shares, experts):
    shares = shares / jnp.sum(shares, axis=-1, keepdims=True)
    matched = picked_ids[:, :, None] == jnp.arange(experts, dtype=jnp.int32)[None, None, :]
    return jnp.sum(jnp.where(matched, shares[:, :, None], 0.0), axis=1)


def make_slots(route_share, slot_count):
    chosen = route_share > 0.0
    counts = chosen.astype(jnp.int32)
    before = jnp.cumsum(counts, axis=-2) - counts
    before = jnp.swapaxes(before, -1, -2)[..., :, None, :]
    chosen_t = jnp.swapaxes(chosen, -1, -2)[..., :, None, :]
    return (before == jnp.arange(slot_count, dtype=jnp.int32)[:, None]) & chosen_t


def local(
    tokens,
    attn_gain,
    moe_gain,
    w_query,
    w_key,
    w_value,
    w_out,
    expert_gate,
    expert_up,
    expert_down,
    routes,
    route_weights,
):
    groups = lax.axis_size("expert")
    column = lax.axis_index("expert")
    rows_here = tokens.shape[1]
    seq_rows = rows_here * groups
    local_cols = w_query.shape[1]
    heads_here = local_cols // HD
    key_heads = w_key.shape[1] // HD
    residual_in = tokens[0].astype(jnp.float32)
    own_rows = rms_norm(residual_in, attn_gain).astype(jnp.bfloat16)
    gathered = lax.all_gather(own_rows, "expert", axis=0, tiled=True)
    key_start = column * key_heads // groups * HD
    positions = jnp.arange(seq_rows, dtype=jnp.float32)
    key_cols = lax.dynamic_slice_in_dim(w_key, key_start, HD, 1)
    value_cols = lax.dynamic_slice_in_dim(w_value, key_start, HD, 1)
    queries = add_rows(gathered, lax.all_gather(w_query, "dp", axis=0, tiled=True))
    key_rows = add_rows(gathered, lax.all_gather(key_cols, "dp", axis=0, tiled=True))
    values = add_rows(gathered, lax.all_gather(value_cols, "dp", axis=0, tiled=True))
    key_rows = (
        rotate(key_rows.reshape(seq_rows, 1, HD), positions)
        .reshape(seq_rows, HD)
        .astype(jnp.bfloat16)
    )
    values = values.astype(jnp.bfloat16)
    queries = rotate(queries.reshape(seq_rows, heads_here, HD), positions).astype(jnp.bfloat16)
    scores = jnp.einsum(
        "qhd,kd->hqk", queries, key_rows, preferred_element_type=jnp.float32
    ) / math.sqrt(HD)
    causal = jnp.arange(seq_rows)[:, None] >= jnp.arange(seq_rows)[None, :]
    scores = jnp.where(causal[None], scores, -1e30)
    scores = scores - jnp.max(scores, axis=-1, keepdims=True)
    exp_scores = jnp.exp(scores)
    probs = (exp_scores / jnp.sum(exp_scores, axis=-1, keepdims=True)).astype(jnp.bfloat16)
    mixed_heads = (
        jnp.einsum("hqk,kd->qhd", probs, values, preferred_element_type=jnp.float32)
        .astype(jnp.bfloat16)
        .reshape(seq_rows, local_cols)
    )
    partial_value = jnp.dot(
        mixed_heads,
        lax.all_gather(w_out, "dp", axis=1, tiled=True),
        preferred_element_type=jnp.float32,
    )
    route_share = share_table(routes[0], route_weights[0], EXPERTS)
    attn_own = lax.psum_scatter(
        partial_value.astype(jnp.bfloat16), "expert", scatter_dimension=0, tiled=True
    ).astype(jnp.float32)
    residual = residual_in + attn_own
    moe_in = rms_norm(residual, moe_gain).astype(jnp.bfloat16)
    slot_masks = make_slots(route_share, CAP)
    slot_rows = jnp.einsum(
        "ect,td->ecd", slot_masks.astype(jnp.bfloat16), moe_in, preferred_element_type=jnp.float32
    ).astype(jnp.bfloat16)
    arrived = lax.all_to_all(slot_rows, "expert", split_axis=0, concat_axis=1, tiled=True)
    produced = run_experts(arrived, expert_gate, expert_up, expert_down)
    returned = lax.all_to_all(produced, "expert", split_axis=1, concat_axis=0, tiled=True)
    picked = jnp.einsum(
        "ect,ecd->ted",
        slot_masks.astype(jnp.bfloat16),
        returned,
        preferred_element_type=jnp.float32,
    )
    expert_mix = jnp.sum(route_share[:, :, None] * picked, axis=1)
    layer_out = residual + expert_mix
    return layer_out.astype(jnp.bfloat16)[None]


def solution(mesh):
    return jax.shard_map(
        local,
        mesh=mesh,
        in_specs=(
            P("dp", "expert", None),
            P(),
            P(),
            P("dp", "expert"),
            P("dp", None),
            P("dp", None),
            P("expert", "dp"),
            P("expert", "dp", None),
            P("expert", "dp", None),
            P("expert", "dp", None),
            P("dp", "expert", None),
            P("dp", "expert", None),
        ),
        out_specs=P("dp", "expert", None),
        check_vma=False,
    )
```

profile of v0, /device:TPU:1, one launch (start us, length us, event | category | flops | bytes accessed | tf_op | source)
XLA Modules:
  0.0 701.5 jit_solution(12630653821359684707)
XLA Ops:
  8.6 2.0 fusion.21
  11.4 1.5 constant_dynamic-slice_fusion.1
  13.6 1.3 iota_compare_fusion
  14.9 2.7 fusion.31
  17.5 35.7 %all-gather.15.cloned.1.call-done = bf16[4096,256]{1,0:T(8,128)(2,1)} async-done(((bf16[256,256]{1,0:T(8,128)(2,1)}), bf16[4096,256]{1,0:T(8,128)(2,1)}) %all-gather.15.cloned.1.call-update) | async-done | bytes 2097168 | tf_op jit(solution)/shard_map/all_gather | solution.py:108
  53.2 76.1 %all-gather.9.cloned.1.call-done = bf16[1024,4096]{1,0:T(8,128)(2,1)} async-done(((bf16[64,4096]{1,0:T(8,128)(2,1)}), bf16[1024,4096]{1,0:T(8,128)(2,1)}) %all-gather.9.cloned.1.call-update) | async-done | bytes 8388624 | tf_op jit(solution)/shard_map/all_gather | solution.py:103
  129.3 6.3 fusion.51
  136.4 33.5 %all-gather.13.cloned.1.call-done = bf16[4096,128]{1,0:T(8,128)(2,1)} async-done(((bf16[256,128]{1,0:T(8,128)(2,1)}), bf16[4096,128]{1,0:T(8,128)(2,1)}) %all-gather.13.cloned.1.call-update) | async-done | bytes 1048592 | tf_op jit(solution)/shard_map/all_gather | solution.py:109
  169.9 6.5 convolution_bitcast_fusion
  176.4 1.3 subtract_convert_fusion.1
  179.0 8.4 %fusion.50 = (f32[2,1024]{1,0:T(2,128)S(1)}, f32[2,1024,1024]{1,2,0:T(8,128)}) fusion(pred[1024,1024]{0,1:T(8,128)(4,1)} %iota_compare_fusion, bf16[1024,1,64]{0,2,1:T(8,128)(2,1)S(1)} %get-tuple-element.12, bf16[1024,1,64]{0,2,1:T(8,128)(2,1)S(1)} %get-tuple-element.11, bf16[1024,2,64]{2,0,1:T(8,128)(2,1)} %get-tuple-element.8, ...), kind=kOutput, calls=%fused_computation.76 | convolution fusion | flops 546833408 | bytes 10231808 | tf_op jit(solution)/shard_map/sub | solution.py:123
  187.4 21.4 %all-gather.11.cloned.1.call-done = bf16[4096,128]{1,0:T(8,128)(2,1)} async-done(((bf16[256,128]{1,0:T(8,128)(2,1)}), bf16[4096,128]{1,0:T(8,128)(2,1)}) %all-gather.11.cloned.1.call-update) | async-done | bytes 1048592 | tf_op jit(solution)/shard_map/all_gather | solution.py:110
  208.8 10.0 %fusion.17 = bf16[128,2,1024]{2,0,1:T(8,128)(2,1)S(1)} fusion(f32[2,1024,1024]{1,2,0:T(8,128)} %get-tuple-element.16, f32[2,1024]{1,0:T(2,128)S(1)} %get-tuple-element.15, bf16[1024,4096]{1,0:T(8,128)(2,1)} %all-gather.9.cloned.1.call-done, bf16[4096,128]{1,0:T(8,128)(2,1)} %all-gather.11.cloned.1.call-done), kind=kOutput, calls=%fused_computation.25 | convolution fusion | flops 1615200256 | bytes 18358272 | tf_op jit(solution)/shard_map/hqk,kd->qhd/dot_general | solution.py:127
  218.8 31.3 %all-gather.17.cloned.1.call-done = bf16[256,4096]{1,0:T(8,128)(2,1)} async-done(((bf16[256,256]{1,0:T(8,128)(2,1)}), bf16[256,4096]{1,0:T(8,128)(2,1)}) %all-gather.17.cloned.1.call-update) | async-done | bytes 2097168 | tf_op jit(solution)/shard_map/all_gather | solution.py:133
  250.1 7.4 %convolution_convert_fusion = bf16[1024,4096]{1,0:T(8,128)(2,1)} fusion(bf16[1024,256]{0,1:T(8,128)(2,1)S(1)} %bitcast.98, bf16[256,4096]{1,0:T(8,128)(2,1)} %all-gather.17.cloned.1.call-done), kind=kOutput, calls=%fused_computation.6 | convolution fusion | flops 2151677952 | bytes 11010048 | tf_op jit(solution)/shard_map/dot_general | solution.py:131
  260.1 84.6 %reduce-scatter.2.cloned.1.call-done = bf16[64,4096]{1,0:T(8,128)(2,1)} async-done(((bf16[1024,4096]{1,0:T(8,128)(2,1)}), bf16[64,4096]{1,0:T(8,128)(2,1)}) %reduce-scatter.2.cloned.1.call-update) | async-done | bytes 524304 | tf_op jit(solution)/shard_map/reduce_scatter | solution.py:137
  344.7 1.3 multiply_reduce_fusion
  346.0 5.6 convolution_convert_fusion.1
  351.6 5.2 all-to-all-start
  356.8 37.0 %all-gather.19.cloned.1.call-done = bf16[1,4096,768]{2,1,0:T(8,128)(2,1)} async-done(((bf16[1,256,768]{2,1,0:T(8,128)(2,1)}), bf16[1,4096,768]{2,1,0:T(8,128)(2,1)}) %all-gather.19.cloned.1.call-update) | async-done | bytes 6291472 | tf_op jit(solution)/shard_map/all_gather | solution.py:45
  393.8 57.5 %all-to-all-done = bf16[16,48,4096]{2,1,0:T(8,128)(2,1)} async-done(((bf16[16,48,4096]{2,1,0:T(8,128)(2,1)}), bf16[16,48,4096]{2,1,0:T(8,128)(2,1)}, u32[]{:S(2)}, u32[]{:S(2)}) %all-to-all-start) | async-done | bytes 6291488 | tf_op jit(solution)/shard_map/all_to_all | solution.py:146
  451.3 9.0 %fusion.6 = f32[768,768]{1,0:T(8,128)S(1)} fusion(bf16[768,4096]{1,0:T(8,128)(2,1)} %bitcast.15, bf16[1,4096,768]{2,1,0:T(8,128)(2,1)} %all-gather.19.cloned.1.call-done), kind=kOutput, calls=%fused_computation.13 | convolution fusion | flops 4831838208 | bytes 14942208 | tf_op jit(solution)/shard_map/ecd,edf->ecf/dot_general | solution.py:42
  460.4 10.1 %multiply_convert_fusion = bf16[768,768]{1,0:T(8,128)(2,1)} fusion(f32[768,768]{1,0:T(8,128)S(1)} %fusion.6, bf16[768,4096]{1,0:T(8,128)(2,1)} %bitcast.15, bf16[1,4096,768]{2,1,0:T(8,128)(2,1)} %all-gather.21.cloned.1.call-done), kind=kOutput, calls=%fused_computation.21 | convolution fusion | flops 4835377152 | bytes 16121856 | tf_op jit(solution)/shard_map/ecd,edf->ecf/dot_general | solution.py:48
  470.5 16.4 %all-gather.23.cloned.1.call-done = bf16[1,768,4096]{2,1,0:T(8,128)(2,1)} async-done(((bf16[1,48,4096]{2,1,0:T(8,128)(2,1)}), bf16[1,768,4096]{2,1,0:T(8,128)(2,1)}) %all-gather.23.cloned.1.call-update) | async-done | bytes 6291472 | tf_op jit(solution)/shard_map/all_gather | solution.py:59
  486.9 7.5 %fusion.8 = bf16[1,768,4096]{2,1,0:T(8,128)(2,1)S(1)} fusion(bf16[768,768]{1,0:T(8,128)(2,1)} %multiply_convert_fusion, bf16[1,768,4096]{2,1,0:T(8,128)(2,1)} %all-gather.23.cloned.1.call-done), kind=kOutput, calls=%fused_computation.15 | convolution fusion | flops 4834983936 | bytes 13762560 | tf_op jit(solution)/shard_map/ecf,efd->ecd/dot_general | solution.py:56
  494.4 32.6 %copy.69 = bf16[1,768,4096]{2,0,1:T(2,128)(2,1)} copy(bf16[1,768,4096]{2,1,0:T(8,128)(2,1)S(1)} %fusion.8) | data formatting | bytes 12582912 | tf_op jit(solution)/shard_map/convert_element_type | solution.py:62
  527.5 40.0 %reduce.1 = bf16[768,4096]{1,0:T(8,128)(2,1)} reduce(bf16[768,1,4096]{2,1,0:T(2,128)(2,1)} %bitcast.95, bf16[]{:T(256)} %broadcast.116), dimensions={1}, to_apply=%bitcast.93.reduce_sub_computation | reduce | bytes 12582914
  567.5 13.0 %reshape.181 = bf16[16,2,98304]{2,1,0:T(2,128)(2,1)} reshape(bf16[768,4096]{1,0:T(8,128)(2,1)} %reduce.1) | data formatting | bytes 12582912
  580.5 79.0 %all_to_all.21 = bf16[16,2,98304]{2,1,0:T(2,128)(2,1)} all-to-all(bf16[16,2,98304]{2,1,0:T(2,128)(2,1)} %reshape.181), channel_id=1, replica_groups=mesh['dp'=16,'expert'=16] {'expert'}, dimensions={0} | all-to-all | bytes 12582912 | tf_op jit(solution)/shard_map/all_to_all | solution.py:148
  659.5 14.4 %reshape.182 = bf16[768,1,4096]{2,1,0:T(2,128)(2,1)} reshape(bf16[16,2,98304]{2,1,0:T(2,128)(2,1)} %all_to_all.21) | data formatting | bytes 12582912
  673.9 14.3 %copy.65 = bf16[1,768,4096]{2,1,0:T(8,128)(2,1)} copy(bf16[1,768,4096]{2,0,1:T(2,128)(2,1)} %bitcast.94) | data formatting | bytes 12582912
  688.2 5.3 fusion.1
  (54 shorter events, 9.4 us)
Async XLA Ops:
  6.5 4.2 copy-start
  6.5 46.6 %all-gather.15.cloned.1.call-start = ((), (), s32[]{:S(2)}) async-start(), calls=%async_computation.6 | async-start | bytes 2228224 | tf_op jit(solution)/shard_map/all_gather | solution.py:108
  7.3 122.0 %all-gather.9.cloned.1.call-start = ((), (), s32[]{:S(2)}) async-start(), calls=%async_computation.3 | async-start | bytes 8912896 | tf_op jit(solution)/shard_map/all_gather | solution.py:103
  10.6 159.2 %all-gather.13.cloned.1.call-start = ((), (), s32[]{:S(2)}) async-start(), calls=%async_computation.5 | async-start | bytes 1114112 | tf_op jit(solution)/shard_map/all_gather | solution.py:109
  11.4 197.5 %all-gather.11.cloned.1.call-start = ((), (), s32[]{:S(2)}) async-start(), calls=%async_computation.4 | async-start | bytes 1114112 | tf_op jit(solution)/shard_map/all_gather | solution.py:110
  12.9 237.2 %all-gather.17.cloned.1.call-start = ((), (), s32[]{:S(2)}) async-start(), calls=%async_computation.7 | async-start | bytes 2228224 | tf_op jit(solution)/shard_map/all_gather | solution.py:133
  13.5 331.2 %reduce-scatter.2.cloned.1.call-start = ((), (), s32[]{:S(2)}) async-start(), calls=%async_computation.8 | async-start | bytes 8912896 | tf_op jit(solution)/shard_map/reduce_scatter | solution.py:137
  136.4 41.4 %copy-start.4 = (f32[1024,64]{1,0:T(8,128)S(1)}, f32[1024,64]{1,0:T(8,128)}, u32[]{:S(2)}) copy-start(f32[1024,64]{1,0:T(8,128)} %get-tuple-element.14) | copy-start | bytes 786436
  257.5 2.3 copy-start.6
  257.5 2.3 copy-start.7
  257.5 87.2 %copy-start.2 = (bf16[1,64,4096]{2,1,0:T(8,128)(2,1)S(1)}, bf16[1,64,4096]{2,1,0:T(8,128)(2,1)}, u32[]{:S(2)}) copy-start(bf16[1,64,4096]{2,1,0:T(8,128)(2,1)} %param.12) | copy-start | bytes 1572868
  257.5 88.5 %copy-start.5 = (f32[4096]{0:T(1024)S(1)}, f32[4096]{0:T(1024)}, u32[]{:S(2)}) copy-start(f32[4096]{0:T(1024)} %param.14) | copy-start | bytes 49156
  257.5 136.3 %all-gather.19.cloned.1.call-start = ((), (), s32[]{:S(2)}) async-start(), calls=%async_computation.9 | async-start | bytes 6684672 | tf_op jit(solution)/shard_map/all_gather | solution.py:45
  258.3 202.1 %all-gather.21.cloned.1.call-start = ((), (), s32[]{:S(2)}) async-start(), calls=%async_computation.10 | async-start | bytes 6684672 | tf_op jit(solution)/shard_map/all_gather | solution.py:51
  259.0 227.9 %all-gather.23.cloned.1.call-start = ((), (), s32[]{:S(2)}) async-start(), calls=%async_computation.11 | async-start | bytes 6684672 | tf_op jit(solution)/shard_map/all_gather | solution.py:59
  351.6 99.7 %all-to-all-start = ((bf16[16,48,4096]{2,1,0:T(8,128)(2,1)}), bf16[16,48,4096]{2,1,0:T(8,128)(2,1)}, u32[]{:S(2)}, u32[]{:S(2)}) async-start(bf16[16,48,4096]{2,1,0:T(8,128)(2,1)} %convolution_convert_fusion.1), calls=%async_computation.1 | async-start | bytes 12582912 | tf_op jit(solution)/shard_map/all_to_all | solution.py:146
  688.2 6.3 copy-start.1
  688.2 5.4 copy-start.3
Sparse Core Ops, SparseCore 0:
  9.2 43.9 all-gather.14
  55.6 73.6 all-gather.8
  131.1 38.7 all-gather.12
  171.6 37.2 all-gather.10
  210.4 39.6 all-gather.16
  257.6 86.9 reduce-scatter.1
  346.5 47.2 all-gather.18
  395.6 44.6 all-gather.20
  442.2 44.6 all-gather.22
where the time goes:
time: 708 us; the launch traced here: 702 us
  waiting for transfers between devices  397 us (56%)
  blocking collectives  79 us (11%)
  local copies, waits for them, and re-layouts  77.9 us (11%)
  matrix products  76.2 us (11%)
  other arithmetic  52.3 us (7%)
  between operations  13.9 us (2%)
    reduce_scatter x1, waiting for transfers between devices, local(): lax.psum_scatter(partial_value.astype(jnp.bfloat16), 'expert', scatter_di...  84.6 us
    all_to_all x1, blocking collectives, local(): lax.all_to_all(produced, 'expert', split_axis=1, concat_axis=0, tiled=True)  79 us
    all_gather x1, waiting for transfers between devices, local(): gathered = lax.all_gather(own_rows, 'expert', axis=0, tiled=True)  76.1 us
    all_to_all x1, waiting for transfers between devices, local(): lax.all_to_all(slot_rows, 'expert', split_axis=0, concat_axis=1, tiled=True)  57.5 us
    unnamed x22, local copies, waits for them, and re-layouts  42.9 us
    unnamed x1, other arithmetic  40 us
    all_gather x1, waiting for transfers between devices, run_experts(): lax.all_gather(gate_shard, 'dp', axis=1, tiled=True)  37 us
    all_gather x1, waiting for transfers between devices, local(): lax.all_gather(w_query, 'dp', axis=0, tiled=True)  35.7 us
  transfers between devices with their start and end apart: 10, of which 9 were waited for; matrix products, arithmetic and copies ran while one was open for 10% of the time, Pallas kernels for 0%

commit v1 on v0

v1 whole, which is shorter than its diff:
```python
import functools
import math

import jax
import jax.numpy as jnp
import numpy as np
from jax import lax
from jax.experimental import pallas as pl
from jax.experimental.pallas import tpu as pltpu
from jax.sharding import PartitionSpec as P

HD = 128
D = 4096
FF = 768
TOK = 64
HALF = 32
SEQ = 1024
EXTRA = 128
MESH = pl.DeviceIdType.MESH
F32 = jnp.float32
BF16 = jnp.bfloat16
MIB = 1 << 20

STEP = (0, 3, 1, 2)


def place():
    index = lax.axis_index("expert")
    x, y = index // 4, index % 4
    return (
        (x, y, lambda first, second: {"expert": first * 4 + second}),
        (y, x, lambda first, second: {"expert": second * 4 + first}),
    )


def turn(coordinate, step):
    return (coordinate + step) % 4


def meet(spots):
    barrier = pltpu.get_barrier_semaphore()
    for first, second, device in spots:
        for step in (1, 3):
            pl.semaphore_signal(
                barrier, inc=1, device_id=device(turn(first, step), second), device_id_type=MESH
            )
    pl.semaphore_wait(barrier, 4)


def remote(source, target, sends, recvs, slot, device):
    copy = pltpu.make_async_remote_copy(
        src_ref=source,
        dst_ref=target,
        send_sem=sends.at[slot],
        recv_sem=recvs.at[slot],
        device_id=device,
        device_id_type=MESH,
    )
    copy.start()
    return copy


class Gather:
    def __init__(self, spots, block, sends, recvs, own, absolute):
        self.spots, self.block, self.sends, self.recvs = spots, block, sends, recvs
        self.own, self.absolute = own, absolute
        self.copies = {}

    def send(self, half, group, lane, source, target, device):
        slot = (half * 5 + group) * 4 + lane
        self.copies[half, group, lane] = remote(
            source, target, self.sends, self.recvs, slot, device
        )

    def first_hop(self):
        for half, (f, s, device) in enumerate(self.spots):
            for lane, step in ((0, 1), (1, 3)):
                target = self.block(0 if self.absolute else 1 + lane, half, s, 0, HALF)
                self.send(half, 4, lane, self.own(half), target, device(turn(f, step), s))
        self.spread(0)

    def spread(self, r, halves=(0, 1)):
        for half in halves:
            f, s, device = self.spots[half]
            mine = self.own(half) if r == 0 else self.block(r, half, s, 0, HALF)
            for lane, step in ((0, 1), (1, 3)):
                self.send(half, r, lane, mine, self.block(r, half, s, 0, HALF), device(f, turn(s, step)))

    def second_hop(self):
        for lane, step in ((0, 1), (1, 3)):
            for half, (f, s, device) in enumerate(self.spots):
                self.copies[half, 4, lane].wait_recv()
                source = self.block(1 + lane, half, s, lane * 16, 16)
                target = source if self.absolute else self.block(3, half, s, lane * 16, 16)
                self.send(half, 4, 2 + lane, source, target, device(turn(f, step), s))
                self.spread(1 + lane, (half,))

    def last_hop(self):
        for half in (0, 1):
            for lane in (2, 3):
                self.copies[half, 4, lane].wait_recv()
            self.spread(3, (half,))

    def forward(self, r):
        for lane, step in ((0, 1), (1, 3)):
            for half, (f, s, device) in enumerate(self.spots):
                self.copies[half, r, lane].wait_recv()
                here = self.block(r, half, turn(s, 4 - step), lane * 16, 16)
                self.send(half, r, 2 + lane, here, here, device(f, turn(s, step)))

    def finish(self, r):
        for half in (0, 1):
            for lane in (2, 3):
                self.copies[half, r, lane].wait_recv()

    def rest(self):
        self.second_hop()
        self.forward(0)
        self.last_hop()
        for r in (1, 2, 3):
            self.forward(r)
        for r in range(4):
            self.finish(r)
        self.drain()

    def drain(self):
        for copy in self.copies.values():
            copy.wait_send()


class Scatter:
    def __init__(self, spots, y_ref, small, large, z_ref, sends, recvs):
        self.spots, self.y, self.small, self.large, self.z = spots, y_ref, small, large, z_ref
        self.sends, self.recvs = sends, recvs
        self.copies = {}

    def send(self, half, group, lane, source, target, device):
        slot = (half * 5 + group) * 4 + lane
        self.copies[half, group, lane] = remote(
            source, target, self.sends, self.recvs, slot, device
        )

    def parts(self, half, group):
        f, s, device = self.spots[half]
        if group < 4:
            return (
                lambda step: self.y.at[group, half, turn(s, step)],
                lambda step: device(f, turn(s, step)),
            )
        return (
            lambda step: self.z.at[half, STEP.index(step)],
            lambda step: device(turn(f, step), s),
        )

    def start(self, group):
        for half in (0, 1):
            block, device = self.parts(half, group)
            for lane, step in ((0, 1), (1, 3)):
                self.send(
                    half, group, lane, block(2).at[pl.ds(lane * 16, 16)], self.small.at[half, group, lane],
                    device(step),
                )

    def middle(self, group):
        for lane, step in ((0, 1), (1, 3)):
            for half in (0, 1):
                block, device = self.parts(half, group)
                self.copies[half, group, lane].wait_recv()
                rows = block(step).at[pl.ds(lane * 16, 16)]
                rows[...] = (rows[...].astype(F32) + self.small[half, group, lane].astype(F32)).astype(BF16)
                self.send(half, group, 2 + lane, block(step), self.large.at[half, group, lane], device(step))

    def arrived(self, half, group):
        for lane in (2, 3):
            self.copies[half, group, lane].wait_recv()
        return self.large[half, group, 0].astype(F32) + self.large[half, group, 1].astype(F32)

    def finish(self, group):
        for half in (0, 1):
            _, s, _ = self.spots[half]
            total = self.arrived(half, group) + self.y[group, half, s].astype(F32)
            self.z[half, group] = total.astype(BF16)

    def total(self, half):
        return self.arrived(half, 4) + self.z[half, 0].astype(F32)

    def drain(self):
        for copy in self.copies.values():
            copy.wait_send()


def normalized(values, gain):
    return values * lax.rsqrt(jnp.mean(values * values, axis=-1, keepdims=True) + 1e-06) * gain


def gather_kernel(
    tokens, gain, routes, weights, gate, up, down,
    out, extra, shard,
    own, sends, recvs, local, packed,
):
    packs = [
        (part.at[:, pl.ds(c * 256, 256)], shard.at[pl.ds(at + c * 256, 256)])
        for part, at in ((gate, 0), (up, FF))
        for c in range(3)
    ]
    packs += [(down.at[:, pl.ds(c * 256, 256)], shard.at[pl.ds(2 * FF + c * 48, 48)]) for c in range(16)]
    packs = [pltpu.make_async_copy(source, target, packed.at[i]) for i, (source, target) in enumerate(packs)]
    for copy in packs:
        copy.start()
    spots = place()
    index = lax.axis_index("expert")
    own[...] = normalized(tokens[...].astype(F32), gain[...]).astype(BF16)
    keep = pltpu.make_async_copy(own, out.at[index], local)
    keep.start()
    meet(spots)

    def block(r, half, second, start, rows):
        f, _, device = spots[half]
        return out.at[device(turn(f, STEP[r]), second)["expert"], pl.ds(half * HALF + start, rows)]

    gather = Gather(spots, block, sends, recvs, lambda half: own.at[pl.ds(half * HALF, HALF)], True)
    gather.first_hop()

    share = weights[...] / jnp.sum(weights[...], axis=-1, keepdims=True)
    high = share.astype(BF16).astype(F32)
    low = share - high
    lanes = lax.broadcasted_iota(jnp.int32, (TOK, EXTRA), 1)
    table = jnp.zeros((TOK, EXTRA), F32)
    for k in range(routes.shape[1]):
        named = routes[:, k : k + 1]
        table += jnp.where(lanes == named, high[:, k : k + 1], 0.0)
        table += jnp.where(lanes == named + 16, low[:, k : k + 1], 0.0)
    extra[...] = table.astype(BF16)

    gather.rest()
    keep.wait()
    for copy in packs:
        copy.wait()


def attend(
    gathered, weights, tokens, cosine, sine, gain, extra,
    residual, everyone,
    x, w, queries, keys, values, mixed, moe_in, y, small, large, z, sends, recvs, out_sends, out_recvs, local,
):
    spots = place()
    load_w = pltpu.make_async_copy(weights, w, local.at[0])
    load_w.start()
    load_x = pltpu.make_async_copy(gathered, x, local.at[1])
    load_x.start()
    meet(spots)
    load_w.wait()
    load_x.wait()

    def rope(part, rows):
        return part * cosine[rows] + pltpu.roll(part, HD // 2, 1) * sine[rows]

    @pl.loop(0, 4)
    def _(i):
        rows = pl.ds(pl.multiple_of(i * 256, 256), 256)
        left = x[pl.ds(i * 4, 4)].reshape(256, D)
        q = jnp.dot(left, w[:, 0:256].reshape(D, 256), preferred_element_type=F32)
        for head in (0, 1):
            queries[head, rows] = rope(q[:, head * HD : (head + 1) * HD], rows).astype(BF16)
        kv = jnp.dot(left, w[:, 256:512].reshape(D, 256), preferred_element_type=F32)
        keys[rows] = rope(kv[:, :HD], rows).astype(BF16)
        values[rows] = kv[:, HD:].astype(BF16)

    for i in range(4):
        many = (i + 1) * 256
        for head in (0, 1):
            scores = lax.dot_general(
                queries[head, i * 256 : many], keys[0:many], (((1,), (1,)), ((), ())), preferred_element_type=F32
            ) * (1.0 / math.sqrt(HD))
            at_row = lax.broadcasted_iota(jnp.int32, (256, many), 0) + i * 256
            at_col = lax.broadcasted_iota(jnp.int32, (256, many), 1)
            scores = jnp.where(at_row >= at_col, scores, -1e30)
            grown = jnp.exp(scores - jnp.max(scores, axis=-1, keepdims=True))
            total = jnp.sum(grown, axis=-1, keepdims=True)
            part = jnp.dot(grown.astype(BF16), values[0:many], preferred_element_type=F32) / total
            mixed[i * 4 : i * 4 + 4, :, head * HD : (head + 1) * HD] = part.astype(BF16).reshape(4, TOK, HD)

    scatter = Scatter(spots, y, small, large, z, sends, recvs)

    def project(r):
        picked = []
        for half, (f, s, device) in enumerate(spots):
            for second in range(4):
                at = device(turn(f, STEP[r]), second)["expert"]
                picked.append(mixed[at, half * HALF : (half + 1) * HALF])
        left = jnp.concatenate(picked, axis=0)

        @pl.loop(0, 16)
        def _(d):
            part = jnp.dot(left, w[d, 512:768], preferred_element_type=F32)
            cols = pl.ds(pl.multiple_of(d * 256, 256), 256)
            y[r, :, :, :, cols] = part.astype(BF16).reshape(2, 4, HALF, 256)

    for r in (3, 2, 1, 0):
        project(r)
        scatter.start(r)
    for r in (3, 2, 1):
        scatter.middle(r)
    scatter.finish(3)
    scatter.start(4)
    scatter.middle(0)
    scatter.finish(2)
    scatter.finish(1)
    scatter.middle(4)
    scatter.finish(0)
    for half in (0, 1):
        rows = slice(half * HALF, (half + 1) * HALF)
        summed = tokens[rows].astype(F32) + scatter.total(half)
        residual[rows] = summed
        moe_in[rows, 0:D] = normalized(summed, gain[...]).astype(BF16)
    moe_in[:, D:] = extra[...]

    def block(r, half, second, start, rows):
        return everyone.at[r, half, second, pl.ds(start, rows)]

    gather = Gather(spots, block, out_sends, out_recvs, lambda half: moe_in.at[pl.ds(half * HALF, HALF)], False)
    gather.first_hop()
    keeps = []
    for half, (_, s, _) in enumerate(spots):
        keeps.append(pltpu.make_async_copy(gather.own(half), block(0, half, s, 0, HALF), local.at[half]))
        keeps[-1].start()
    scatter.drain()
    gather.rest()
    for keep in keeps:
        keep.wait()


def experts(
    everyone, weights, residual,
    out,
    g, w, act, y, small, large, z, sends, recvs, load_g, load_w, load_down,
):
    spots = place()
    rows_of = [pltpu.make_async_copy(everyone.at[r], g.at[r], load_g.at[r]) for r in range(4)]
    feeds = []
    for c in range(6):
        part = (c // 2 + c % 2 * 3) * 256
        view = pl.ds(part, 256)
        feeds.append(pltpu.make_async_copy(weights.at[:, view], w.at[:, view], load_w.at[c]))
    view = pl.ds(2 * FF, FF)
    downs = pltpu.make_async_copy(weights.at[:, view], w.at[:, view], load_down)
    rows_of[3].start()
    for copy in feeds:
        copy.start()
    for r in (2, 1, 0):
        rows_of[r].start()
    downs.start()
    meet(spots)
    scatter = Scatter(spots, y, small, large, z, sends, recvs)
    index = lax.axis_index("expert")

    def feed_part(r, c):
        cols = pl.ds(c * 256, 256)
        left = g[r, :, :, :, 0:D].reshape(256, D)
        gate = jnp.dot(left, w[:, cols].reshape(D, 256), preferred_element_type=F32)
        up = jnp.dot(left, w[:, pl.ds(FF + c * 256, 256)].reshape(D, 256), preferred_element_type=F32)
        act[:, cols] = (gate / (1.0 + jnp.exp(-gate)) * up).astype(BF16)

    def feed(r):
        rows_of[r].wait()
        for c in range(3):
            if r == 3:
                feeds[2 * c].wait()
                feeds[2 * c + 1].wait()
            feed_part(r, c)

    def down(r):
        table = g[r, :, :, :, D:].reshape(256, EXTRA).astype(F32)
        lanes = lax.broadcasted_iota(jnp.int32, (256, EXTRA), 1)
        chosen = (lanes == index) | (lanes == index + 16)
        share = jnp.sum(jnp.where(chosen, table, 0.0), axis=-1, keepdims=True)

        @pl.loop(0, 16)
        def _(n):
            right = w[:, pl.ds(pl.multiple_of(2 * FF + n * 48, 16), 48)].reshape(FF, 256)
            part = jnp.dot(act[...], right, preferred_element_type=F32) * share
            cols = pl.ds(pl.multiple_of(n * 256, 256), 256)
            y[r, :, :, :, cols] = part.astype(BF16).reshape(2, 4, HALF, 256)

    feed(3)
    downs.wait()
    down(3)
    scatter.start(3)
    feed(2)
    down(2)
    scatter.start(2)
    scatter.middle(3)
    feed(1)
    down(1)
    scatter.start(1)
    scatter.middle(2)
    scatter.finish(3)
    scatter.start(4)
    feed(0)
    scatter.middle(1)
    scatter.finish(2)
    down(0)
    scatter.start(0)
    scatter.finish(1)
    scatter.middle(4)
    scatter.middle(0)
    scatter.finish(0)
    for half in (0, 1):
        rows = slice(half * HALF, (half + 1) * HALF)
        out[rows] = (residual[rows] + scatter.total(half)).astype(BF16)
    scatter.drain()


def rope_tables():
    frequency = np.exp(np.arange(HD // 2, dtype=np.float32) * np.float32(-2.0 * math.log(1000000.0) / HD))
    angles = (np.arange(SEQ, dtype=np.float32)[:, None] * frequency[None, :]).astype(np.float32)
    cosine, sine = np.cos(angles), np.sin(angles)
    return (
        np.concatenate([cosine, cosine], axis=1).astype(np.float32),
        np.concatenate([-sine, sine], axis=1).astype(np.float32),
    )


VMEM = pl.BlockSpec(memory_space=pltpu.VMEM)
ANY = pl.BlockSpec(memory_space=pl.ANY)
HBM = pl.BlockSpec(memory_space=pltpu.HBM)
SEMS = pltpu.SemaphoreType.DMA((40,))
RING = [
    pltpu.VMEM((4, 2, 4, HALF, D), BF16),
    pltpu.VMEM((2, 5, 2, 16, D), BF16),
    pltpu.VMEM((2, 5, 2, HALF, D), BF16),
    pltpu.VMEM((2, 4, HALF, D), BF16),
]


def params(number, mib):
    return pltpu.CompilerParams(collective_id=number, has_side_effects=True, vmem_limit_bytes=mib * MIB)


def cost(flops, moved):
    return pl.CostEstimate(flops=flops, bytes_accessed=moved, transcendentals=0)


def local(
    tokens,
    attn_gain,
    moe_gain,
    w_query,
    w_key,
    w_value,
    w_out,
    expert_gate,
    expert_up,
    expert_down,
    routes,
    route_weights,
):
    groups = lax.axis_size("expert")
    column = lax.axis_index("expert")
    key_heads = w_key.shape[1] // HD
    key_start = column * key_heads // groups * HD
    rows = tokens[0]
    key_cols = lax.dynamic_slice_in_dim(w_key, key_start, HD, 1)
    value_cols = lax.dynamic_slice_in_dim(w_value, key_start, HD, 1)
    attn_shard = jnp.concatenate([w_query, jnp.concatenate([key_cols, value_cols], axis=1), w_out], axis=0)
    attn_weights = lax.all_gather(attn_shard, "dp", axis=0)
    gathered, extra, moe_shard = pl.pallas_call(
        gather_kernel,
        out_shape=(
            jax.ShapeDtypeStruct((16, TOK, D), BF16),
            jax.ShapeDtypeStruct((TOK, EXTRA), BF16),
            jax.ShapeDtypeStruct((2304, 256), BF16),
        ),
        in_specs=[VMEM] * 4 + [ANY] * 3,
        out_specs=(HBM, VMEM, HBM),
        scratch_shapes=[
            pltpu.VMEM((TOK, D), BF16),
            SEMS,
            SEMS,
            pltpu.SemaphoreType.DMA,
            pltpu.SemaphoreType.DMA((22,)),
        ],
        compiler_params=params(0, 60),
        cost_estimate=cost(1 << 22, 100 * MIB),
        name="gather_tokens",
    )(rows, attn_gain[None], routes[0], route_weights[0], expert_gate[0], expert_up[0], expert_down[0])

    moe_shard, attn_weights = lax.optimization_barrier((moe_shard, attn_weights))
    moe_weights = lax.all_gather(moe_shard, "dp", axis=0)
    cosine, sine = rope_tables()

    residual, everyone = pl.pallas_call(
        attend,
        out_shape=(
            jax.ShapeDtypeStruct((TOK, D), F32),
            jax.ShapeDtypeStruct((4, 2, 4, HALF, D + EXTRA), BF16),
        ),
        in_specs=[ANY, ANY, VMEM, VMEM, VMEM, VMEM, VMEM],
        out_specs=(VMEM, HBM),
        scratch_shapes=[
            pltpu.VMEM((16, TOK, D), BF16),
            pltpu.VMEM((16, 768, 256), BF16),
            pltpu.VMEM((2, SEQ, HD), BF16),
            pltpu.VMEM((SEQ, HD), BF16),
            pltpu.VMEM((SEQ, HD), BF16),
            pltpu.VMEM((16, TOK, 256), BF16),
            pltpu.VMEM((TOK, D + EXTRA), BF16),
            *RING,
            SEMS,
            SEMS,
            SEMS,
            SEMS,
            pltpu.SemaphoreType.DMA((2,)),
        ],
        compiler_params=params(1, 56),
        cost_estimate=cost(8 << 30, 150 * MIB),
        name="attention",
    )(gathered, attn_weights, rows, cosine, sine, moe_gain[None], extra)

    layer_out = pl.pallas_call(
        experts,
        out_shape=jax.ShapeDtypeStruct((TOK, D), BF16),
        in_specs=[ANY, ANY, VMEM],
        out_specs=VMEM,
        scratch_shapes=[
            pltpu.VMEM((4, 2, 4, HALF, D + EXTRA), BF16),
            pltpu.VMEM((16, 2304, 256), BF16),
            pltpu.VMEM((256, FF), BF16),
            *RING,
            SEMS,
            SEMS,
            pltpu.SemaphoreType.DMA((4,)),
            pltpu.SemaphoreType.DMA((6,)),
            pltpu.SemaphoreType.DMA,
        ],
        compiler_params=params(2, 60),
        cost_estimate=cost(20 << 30, 200 * MIB),
        name="experts",
    )(everyone, moe_weights, residual)
    return layer_out[None]


def solution(mesh):
    return jax.shard_map(
        local,
        mesh=mesh,
        in_specs=(
            P("dp", "expert", None),
            P(),
            P(),
            P("dp", "expert"),
            P("dp", None),
            P("dp", None),
            P("expert", "dp"),
            P("expert", "dp", None),
            P("expert", "dp", None),
            P("expert", "dp", None),
            P("dp", "expert", None),
            P("dp", "expert", None),
        ),
        out_specs=P("dp", "expert", None),
        check_vma=False,
    )
```

time: 708 us -> 251 us (0.35)
  waiting for transfers between devices: 397 us -> 0.08 us
  Pallas kernels: 0 us -> 228 us
  blocking collectives: 79 us -> 0 us
  matrix products: 76.2 us -> 0 us
  local copies, waits for them, and re-layouts: 77.9 us -> 5.51 us
  other arithmetic: 52.3 us -> 1.75 us
    all_gather x8 -> x2, waiting for transfers between devices: 251 us -> 0.04 us  [the longest x1 0.02 us: local(): moe_weights = lax.all_gather(moe_shard, 'dp', axis=0)]
    pallas_call x0 -> x3, Pallas kernels: none -> 228 us  [the longest x1 113 us: local(): pl.pallas_call(attend, out_shape=(jax.ShapeDtypeStruct((TOK, D), F32), ja...]
    reduce_scatter x1 -> x0, waiting for transfers between devices: 84.6 us -> none  [local(): lax.psum_scatter(partial_value.astype(jnp.bfloat16), 'expert', scatter_di...]
    all_to_all x1 -> x0, blocking collectives: 79 us -> none  [local(): lax.all_to_all(produced, 'expert', split_axis=1, concat_axis=0, tiled=True)]
    dot_general x9 -> x0, matrix products: 67.8 us -> none  [the longest x2 12.9 us: add_rows(): return jnp.dot(left_rows, pieces, preferred_element_type=jnp.float32)]
    all_to_all x1 -> x0, waiting for transfers between devices: 57.5 us -> none  [local(): lax.all_to_all(slot_rows, 'expert', split_axis=0, concat_axis=1, tiled=True)]
    unnamed x1 -> x0, other arithmetic: 40 us -> none
    unnamed x22 -> x3, local copies, waits for them, and re-layouts: 42.9 us -> 4.63 us
  transfers between devices with their start and end apart: 10 -> 2, of which waited for: 9 -> 0; matrix products, arithmetic and copies ran while one was open for 10% -> 1% of each run, Pallas kernels for 0% -> 66%
where the time goes in v1:
time: 251 us; the launch traced here: 249 us
  Pallas kernels  228 us (91%)
  between operations  13.4 us (5%)
  local copies, waits for them, and re-layouts  5.51 us (2%)
    pallas_call x1, Pallas kernels, local(): pl.pallas_call(attend, out_shape=(jax.ShapeDtypeStruct((TOK, D), F32), ja...  113 us
    pallas_call x1, Pallas kernels, local(): pl.pallas_call(experts, out_shape=jax.ShapeDtypeStruct((TOK, D), BF16), i...  63.8 us
    pallas_call x1, Pallas kernels, local(): pl.pallas_call(gather_kernel, out_shape=(jax.ShapeDtypeStruct((16, TOK, D...  51.3 us
  transfers between devices with their start and end apart: 2, of which 0 were waited for; matrix products, arithmetic and copies ran while one was open for 1% of the time, Pallas kernels for 66%

profile of v1, /device:TPU:1, one launch (start us, length us, event | category | flops | bytes accessed | tf_op | source)
XLA Modules:
  0.0 249.2 jit_solution(11024284016770481132)
XLA Ops:
  6.5 0.0 all-gather.5.cloned.1.call-start
  6.5 0.9 constant_dynamic-slice_fusion
  7.4 1.7 pad_maximum_fusion
  9.2 0.0 all-gather.5.cloned.1.call-update
  9.2 0.0 all-gather.7.cloned.1.call-start
  9.2 1.4 copy.15
  10.6 1.4 copy.16
  12.0 51.3 %gather_tokens.1 = (bf16[16,64,4096]{2,1,0:T(8,128)(2,1)}, bf16[64,128]{1,0:T(8,128)(2,1)}, bf16[2304,256]{1,0:T(8,128)(2,1)}) custom-call(bf16[64,4096]{1,0:T(8,128)(2,1)} %bitcast.11, f32[1,4096]{1,0:T(1,128)} %bitcast.19, s32[64,8]{1,0:T(8,128)} %bitcast.17, f32[64,8]{1,0:T(8,128)} %bitcast.18, bf16[256,768]{1,0:T(8,128)(2,1)} %bitcast.14, ...), custom_call_target="tpu_custom_call" | custom-call | flops 4194304 | bytes 104857600 | tf_op jit(solution)/shard_map/gather_tokens/pallas_call | solution.py:467
  63.3 0.0 all-gather.5.cloned.1.call-done
  63.4 0.0 all-gather.7.cloned.1.call-update
  63.4 113.3 %attention.1 = (f32[64,4096]{1,0:T(8,128)}, bf16[4,2,4,32,4224]{4,3,2,1,0:T(8,128)(2,1)}) custom-call(bf16[16,64,4096]{2,1,0:T(8,128)(2,1)} %get-tuple-element.12.gathered, bf16[16,768,256]{2,1,0:T(8,128)(2,1)} %bitcast.21, bf16[64,4096]{1,0:T(8,128)(2,1)} %bitcast.12, f32[1024,128]{1,0:T(8,128)} %constant.31.clone.cosine, f32[1024,128]{1,0:T(8,128)} %constant.32.clone.sine, ...), custom_call_target="tpu_custom_call" | custom-call | flops 8589934592 | bytes 157286400 | tf_op jit(solution)/shard_map/attention/pallas_call | solution.py:492
  176.7 0.0 all-gather.7.cloned.1.call-done
  176.7 63.8 %experts.1 = bf16[64,4096]{1,0:T(8,128)(2,1)} custom-call(bf16[4,2,4,32,4224]{4,3,2,1,0:T(8,128)(2,1)} %get-tuple-element.16.everyone, bf16[16,2304,256]{2,1,0:T(8,128)(2,1)} %bitcast.20, f32[64,4096]{1,0:T(8,128)} %get-tuple-element.18.residual), custom_call_target="tpu_custom_call" | custom-call | flops 21474836480 | bytes 209715200 | tf_op jit(solution)/shard_map/experts/pallas_call | solution.py:520
  240.5 1.9 copy.18
Async XLA Ops:
  6.5 56.8 %all-gather.5.cloned.1.call-start = ((), (), s32[]{:S(2)}) async-start(), calls=%async_computation | async-start | bytes 6684672 | tf_op jit(solution)/shard_map/all_gather | solution.py:466
  9.2 167.5 %all-gather.7.cloned.1.call-start = ((), (), s32[]{:S(2)}) async-start(), calls=%async_computation.1 | async-start | bytes 20054016 | tf_op jit(solution)/shard_map/all_gather | solution.py:489
Sparse Core Ops, SparseCore 0:
  9.3 52.8 all-gather.4
  64.0 109.5 all-gather.6

commit v2 on v1

--- a/solution.py
+++ b/solution.py
@@ -37,14 +37,15 @@
     return (coordinate + step) % 4
 
 
-def meet(spots):
+def around(spots):
+    return [device(turn(f, step), s) for f, s, device in spots for step in (1, 3)]
+
+
+def meet(devices):
     barrier = pltpu.get_barrier_semaphore()
-    for first, second, device in spots:
-        for step in (1, 3):
-            pl.semaphore_signal(
-                barrier, inc=1, device_id=device(turn(first, step), second), device_id_type=MESH
-            )
-    pl.semaphore_wait(barrier, 4)
+    for device in devices:
+        pl.semaphore_signal(barrier, inc=1, device_id=device, device_id_type=MESH)
+    pl.semaphore_wait(barrier, len(devices))
 
 
 def remote(source, target, sends, recvs, slot, device):
@@ -129,9 +130,9 @@
 
 
 class Scatter:
-    def __init__(self, spots, y_ref, small, large, z_ref, sends, recvs):
+    def __init__(self, spots, y_ref, small, large, z_ref, sends, recvs, cut=HALF // 2):
         self.spots, self.y, self.small, self.large, self.z = spots, y_ref, small, large, z_ref
-        self.sends, self.recvs = sends, recvs
+        self.sends, self.recvs, self.cut = sends, recvs, cut
         self.copies = {}
 
     def send(self, half, group, lane, source, target, device):
@@ -157,7 +158,7 @@
             block, device = self.parts(half, group)
             for lane, step in ((0, 1), (1, 3)):
                 self.send(
-                    half, group, lane, block(2).at[pl.ds(lane * 16, 16)], self.small.at[half, group, lane],
+                    half, group, lane, block(2).at[pl.ds(lane * self.cut, self.cut)], self.small.at[half, group, lane],
                     device(step),
                 )
 
@@ -166,7 +167,7 @@
             for half in (0, 1):
                 block, device = self.parts(half, group)
                 self.copies[half, group, lane].wait_recv()
-                rows = block(step).at[pl.ds(lane * 16, 16)]
+                rows = block(step).at[pl.ds(lane * self.cut, self.cut)]
                 rows[...] = (rows[...].astype(F32) + self.small[half, group, lane].astype(F32)).astype(BF16)
                 self.send(half, group, 2 + lane, block(step), self.large.at[half, group, lane], device(step))
 
@@ -189,30 +190,44 @@
             copy.wait_send()
 
 
+class Fold(Scatter):
+    def parts(self, half, group):
+        f, s, device = self.spots[half]
+        return (lambda step: self.y.at[half, turn(f, step)], lambda step: device(turn(f, step), s))
+
+    def total(self, half):
+        return self.arrived(half, 0) + self.y[half, self.spots[half][0]].astype(F32)
+
+
 def normalized(values, gain):
     return values * lax.rsqrt(jnp.mean(values * values, axis=-1, keepdims=True) + 1e-06) * gain
 
 
+def pack_kernel(gate, up, down, w_query, w_key, w_value, w_out, attn_shard, moe_shard):
+    key_cols = pl.ds(pl.multiple_of(lax.axis_index("expert") // 8 * HD, HD), HD)
+    attn_shard[0:256] = w_query[...]
+    attn_shard[256:512, 0:HD] = w_key[:, key_cols]
+    attn_shard[256:512, HD:] = w_value[:, key_cols]
+    attn_shard[512:768] = w_out[...]
+    for c in range(3):
+        cols = slice(c * 256, c * 256 + 256)
+        moe_shard[cols] = gate[:, cols]
+        moe_shard[FF + c * 256 : FF + c * 256 + 256] = up[:, cols]
+    for c in range(16):
+        moe_shard[2 * FF + c * 48 : 2 * FF + c * 48 + 48] = down[:, c * 256 : c * 256 + 256]
+
+
 def gather_kernel(
-    tokens, gain, routes, weights, gate, up, down,
-    out, extra, shard,
-    own, sends, recvs, local, packed,
+    tokens, gain, routes, weights,
+    out, extra,
+    own, sends, recvs, local,
 ):
-    packs = [
-        (part.at[:, pl.ds(c * 256, 256)], shard.at[pl.ds(at + c * 256, 256)])
-        for part, at in ((gate, 0), (up, FF))
-        for c in range(3)
-    ]
-    packs += [(down.at[:, pl.ds(c * 256, 256)], shard.at[pl.ds(2 * FF + c * 48, 48)]) for c in range(16)]
-    packs = [pltpu.make_async_copy(source, target, packed.at[i]) for i, (source, target) in enumerate(packs)]
-    for copy in packs:
-        copy.start()
     spots = place()
     index = lax.axis_index("expert")
     own[...] = normalized(tokens[...].astype(F32), gain[...]).astype(BF16)
     keep = pltpu.make_async_copy(own, out.at[index], local)
     keep.start()
-    meet(spots)
+    meet(around(spots))
 
     def block(r, half, second, start, rows):
         f, _, device = spots[half]
@@ -221,44 +236,100 @@
     gather = Gather(spots, block, sends, recvs, lambda half: own.at[pl.ds(half * HALF, HALF)], True)
     gather.first_hop()
 
-    share = weights[...] / jnp.sum(weights[...], axis=-1, keepdims=True)
+    share = weights[...] / jnp.sum(weights[...], axis=0, keepdims=True)
     high = share.astype(BF16).astype(F32)
     low = share - high
-    lanes = lax.broadcasted_iota(jnp.int32, (TOK, EXTRA), 1)
-    table = jnp.zeros((TOK, EXTRA), F32)
-    for k in range(routes.shape[1]):
-        named = routes[:, k : k + 1]
-        table += jnp.where(lanes == named, high[:, k : k + 1], 0.0)
-        table += jnp.where(lanes == named + 16, low[:, k : k + 1], 0.0)
-    extra[...] = table.astype(BF16)
+    at_row = lax.broadcasted_iota(jnp.int32, (EXTRA, TOK), 0)
+    table = jnp.zeros((EXTRA, TOK), F32)
+    for k in range(routes.shape[0]):
+        named = routes[k : k + 1]
+        table += jnp.where(at_row == named, high[k : k + 1], 0.0)
+        table += jnp.where(at_row == named + 16, low[k : k + 1], 0.0)
+    extra[...] = table.T.astype(BF16)
 
     gather.rest()
     keep.wait()
-    for copy in packs:
-        copy.wait()
+
+
+class Share:
+    def __init__(self, spots, weights, wo, sends, recvs):
+        index = lax.axis_index("dp")
+        self.core = index % 2
+        self.other = {"dp": index + 1 - 2 * self.core}
+        self.spots, self.weights, self.wo, self.sends, self.recvs = spots, weights, wo, sends, recvs
+        self.copies = {}
+
+    def block(self, half, second, start, count):
+        return self.wo.at[half, pl.ds(4 * self.core + start, count), second]
+
+    def send(self, half, lane, source, target, device):
+        self.copies[half, lane] = remote(source, target, self.sends, self.recvs, half * 8 + lane, device)
+
+    def start(self):
+        for half, (f, s, device) in enumerate(self.spots):
+            source = self.weights.at[pl.ds(8 * half + 4 * self.core, 4), pl.ds(512, 256)]
+            for lane, step in ((0, 1), (1, 3)):
+                self.send(half, lane, source, self.block(half, s, 0, 4), device(f, turn(s, step)))
+
+    def forward(self):
+        for lane, step in ((0, 1), (1, 3)):
+            for half, (f, s, device) in enumerate(self.spots):
+                self.copies[half, lane].wait_recv()
+                here = self.block(half, turn(s, 4 - step), 2 * lane, 2)
+                self.send(half, 2 + lane, here, here, device(f, turn(s, step)))
+                here = self.block(half, turn(s, 4 - step), 0, 4)
+                self.send(half, 4 + lane, here, here, self.other)
+
+    def finish(self):
+        for lane in (0, 1):
+            for half, (f, s, device) in enumerate(self.spots):
+                self.copies[half, 2 + lane].wait_recv()
+                here = self.block(half, turn(s, 2), 2 * lane, 2)
+                self.send(half, 6 + lane, here, here, self.other)
+
+    def arrive(self):
+        for half in (0, 1):
+            for lane in range(4, 8):
+                self.copies[half, lane].wait_recv()
+
+    def drain(self):
+        for copy in self.copies.values():
+            copy.wait_send()
 
 
 def attend(
     gathered, weights, tokens, cosine, sine, gain, extra,
     residual, everyone,
-    x, w, queries, keys, values, mixed, moe_in, y, small, large, z, sends, recvs, out_sends, out_recvs, local,
+    x, w, wo, queries, keys, values, mixed, mx, moe_in, y, small, large,
+    wo_sends, wo_recvs, mx_sends, mx_recvs, sends, recvs, out_sends, out_recvs, local,
 ):
     spots = place()
-    load_w = pltpu.make_async_copy(weights, w, local.at[0])
+    load_w = pltpu.make_async_copy(weights.at[:, pl.ds(0, 512)], w, local.at[0])
     load_w.start()
-    load_x = pltpu.make_async_copy(gathered, x, local.at[1])
-    load_x.start()
-    meet(spots)
+    loads = []
+    for i in range(4):
+        loads.append(pltpu.make_async_copy(gathered.at[pl.ds(i * 4, 4)], x.at[pl.ds(i * 4, 4)], local.at[1 + i]))
+        loads[-1].start()
+    for half, (f, s, _) in enumerate(spots):
+        loads.append(
+            pltpu.make_async_copy(
+                weights.at[pl.ds(8 * half, 8), pl.ds(512, 256)], wo.at[half, :, s], local.at[5 + half]
+            )
+        )
+        loads[-1].start()
+    share = Share(spots, weights, wo, wo_sends, wo_recvs)
+    across = [device(f, turn(s, 2)) for f, s, device in spots]
+    meet(around(spots) + across + [share.other])
+    share.start()
     load_w.wait()
-    load_x.wait()
 
     def rope(part, rows):
         return part * cosine[rows] + pltpu.roll(part, HD // 2, 1) * sine[rows]
 
-    @pl.loop(0, 4)
-    def _(i):
-        rows = pl.ds(pl.multiple_of(i * 256, 256), 256)
-        left = x[pl.ds(i * 4, 4)].reshape(256, D)
+    def project(i):
+        loads[i].wait()
+        rows = slice(i * 256, i * 256 + 256)
+        left = x[i * 4 : i * 4 + 4].reshape(256, D)
         q = jnp.dot(left, w[:, 0:256].reshape(D, 256), preferred_element_type=F32)
         for head in (0, 1):
             queries[head, rows] = rope(q[:, head * HD : (head + 1) * HD], rows).astype(BF16)
@@ -266,7 +337,7 @@
         keys[rows] = rope(kv[:, :HD], rows).astype(BF16)
         values[rows] = kv[:, HD:].astype(BF16)
 
-    for i in range(4):
+    def attention(i):
         many = (i + 1) * 256
         for head in (0, 1):
             scores = lax.dot_general(
@@ -278,41 +349,58 @@
             grown = jnp.exp(scores - jnp.max(scores, axis=-1, keepdims=True))
             total = jnp.sum(grown, axis=-1, keepdims=True)
             part = jnp.dot(grown.astype(BF16), values[0:many], preferred_element_type=F32) / total
-            mixed[i * 4 : i * 4 + 4, :, head * HD : (head + 1) * HD] = part.astype(BF16).reshape(4, TOK, HD)
-
-    scatter = Scatter(spots, y, small, large, z, sends, recvs)
-
-    def project(r):
-        picked = []
+            mixed[i, :, :, head * HD : (head + 1) * HD] = part.astype(BF16).reshape(4, TOK, HD)
+
+    for i in range(4):
+        project(i)
+    share.forward()
+    for i in range(4):
+        attention(i)
+
+    def rows_of(half, second):
+        return mixed.at[second] if half else mixed.at[:, second]
+
+    swaps = []
+    for i, step in enumerate((1, 3, 2)):
         for half, (f, s, device) in enumerate(spots):
-            for second in range(4):
-                at = device(turn(f, STEP[r]), second)["expert"]
-                picked.append(mixed[at, half * HALF : (half + 1) * HALF])
-        left = jnp.concatenate(picked, axis=0)
-
-        @pl.loop(0, 16)
-        def _(d):
-            part = jnp.dot(left, w[d, 512:768], preferred_element_type=F32)
-            cols = pl.ds(pl.multiple_of(d * 256, 256), 256)
-            y[r, :, :, :, cols] = part.astype(BF16).reshape(2, 4, HALF, 256)
-
-    for r in (3, 2, 1, 0):
-        project(r)
-        scatter.start(r)
-    for r in (3, 2, 1):
-        scatter.middle(r)
-    scatter.finish(3)
-    scatter.start(4)
-    scatter.middle(0)
-    scatter.finish(2)
-    scatter.finish(1)
-    scatter.middle(4)
-    scatter.finish(0)
+            cols = pl.ds(pl.multiple_of(s * 256, 256), 256)
+            to = turn(s, step)
+            swaps.append(
+                remote(rows_of(half, to), mx.at[half, :, :, cols], mx_sends, mx_recvs, half * 3 + i, device(f, to))
+            )
+    keeps = []
+    for half, (f, s, device) in enumerate(spots):
+        cols = pl.ds(pl.multiple_of(s * 256, 256), 256)
+        keeps.append(pltpu.make_async_copy(rows_of(half, s), mx.at[half, :, :, cols], local.at[half]))
+        keeps[-1].start()
+    share.finish()
+    for copy in keeps + loads[4:]:
+        copy.wait()
+    for copy in swaps:
+        copy.wait_recv()
+    share.arrive()
+
+    fold = Fold(spots, y, small, large, None, sends, recvs, HALF)
     for half in (0, 1):
-        rows = slice(half * HALF, (half + 1) * HALF)
-        summed = tokens[rows].astype(F32) + scatter.total(half)
-        residual[rows] = summed
-        moe_in[rows, 0:D] = normalized(summed, gain[...]).astype(BF16)
+
+        @pl.loop(0, 2)
+        def _(group):
+            left = mx[half].reshape(256, 1024)
+            for c in range(4):
+                right = wo[half, group * 4 + c].reshape(1024, 256)
+                part = jnp.dot(left, right, preferred_element_type=F32)
+                cols = pl.ds(pl.multiple_of(group * 1024 + c * 256, 256), 256)
+                y[half, :, :, cols] = part.astype(BF16).reshape(4, TOK, 256)
+
+    fold.start(0)
+    for copy in swaps:
+        copy.wait_send()
+    share.drain()
+    fold.middle(0)
+    for half in (0, 1):
+        cols = slice(half * 2048, (half + 1) * 2048)
+        residual[:, cols] = tokens[:, cols].astype(F32) + fold.total(half)
+    moe_in[:, 0:D] = normalized(residual[...], gain[...]).astype(BF16)
     moe_in[:, D:] = extra[...]
 
     def block(r, half, second, start, rows):
@@ -324,7 +412,7 @@
     for half, (_, s, _) in enumerate(spots):
         keeps.append(pltpu.make_async_copy(gather.own(half), block(0, half, s, 0, HALF), local.at[half]))
         keeps[-1].start()
-    scatter.drain()
+    fold.drain()
     gather.rest()
     for keep in keeps:
         keep.wait()
@@ -350,7 +438,7 @@
     for r in (2, 1, 0):
         rows_of[r].start()
     downs.start()
-    meet(spots)
+    meet(around(spots))
     scatter = Scatter(spots, y, small, large, z, sends, recvs)
     index = lax.axis_index("expert")
 
@@ -375,12 +463,14 @@
         chosen = (lanes == index) | (lanes == index + 16)
         share = jnp.sum(jnp.where(chosen, table, 0.0), axis=-1, keepdims=True)
 
-        @pl.loop(0, 16)
-        def _(n):
-            right = w[:, pl.ds(pl.multiple_of(2 * FF + n * 48, 16), 48)].reshape(FF, 256)
-            part = jnp.dot(act[...], right, preferred_element_type=F32) * share
-            cols = pl.ds(pl.multiple_of(n * 256, 256), 256)
-            y[r, :, :, :, cols] = part.astype(BF16).reshape(2, 4, HALF, 256)
+        @pl.loop(0, 4)
+        def _(group):
+            for c in range(4):
+                n = group * 4 + c
+                right = w[:, pl.ds(pl.multiple_of(2 * FF + n * 48, 16), 48)].reshape(FF, 256)
+                part = jnp.dot(act[...], right, preferred_element_type=F32) * share
+                cols = pl.ds(pl.multiple_of(n * 256, 256), 256)
+                y[r, :, :, :, cols] = part.astype(BF16).reshape(2, 4, HALF, 256)
 
     feed(3)
     downs.wait()
@@ -455,40 +545,31 @@
     routes,
     route_weights,
 ):
-    groups = lax.axis_size("expert")
-    column = lax.axis_index("expert")
-    key_heads = w_key.shape[1] // HD
-    key_start = column * key_heads // groups * HD
     rows = tokens[0]
-    key_cols = lax.dynamic_slice_in_dim(w_key, key_start, HD, 1)
-    value_cols = lax.dynamic_slice_in_dim(w_value, key_start, HD, 1)
-    attn_shard = jnp.concatenate([w_query, jnp.concatenate([key_cols, value_cols], axis=1), w_out], axis=0)
+    attn_shard, moe_shard = pl.pallas_call(
+        pack_kernel,
+        out_shape=(jax.ShapeDtypeStruct((768, 256), BF16), jax.ShapeDtypeStruct((2304, 256), BF16)),
+        in_specs=[VMEM] * 7,
+        out_specs=(VMEM, VMEM),
+        compiler_params=pltpu.CompilerParams(vmem_limit_bytes=60 * MIB),
+        cost_estimate=cost(1 << 10, 4 * MIB),
+        name="pack_weights",
+    )(expert_gate[0], expert_up[0], expert_down[0], w_query, w_key, w_value, w_out)
     attn_weights = lax.all_gather(attn_shard, "dp", axis=0)
-    gathered, extra, moe_shard = pl.pallas_call(
+    moe_weights = lax.all_gather(moe_shard, "dp", axis=0)
+
+    gathered, extra = pl.pallas_call(
         gather_kernel,
-        out_shape=(
-            jax.ShapeDtypeStruct((16, TOK, D), BF16),
-            jax.ShapeDtypeStruct((TOK, EXTRA), BF16),
-            jax.ShapeDtypeStruct((2304, 256), BF16),
-        ),
-        in_specs=[VMEM] * 4 + [ANY] * 3,
-        out_specs=(HBM, VMEM, HBM),
-        scratch_shapes=[
-            pltpu.VMEM((TOK, D), BF16),
-            SEMS,
-            SEMS,
-            pltpu.SemaphoreType.DMA,
-            pltpu.SemaphoreType.DMA((22,)),
-        ],
+        out_shape=(jax.ShapeDtypeStruct((16, TOK, D), BF16), jax.ShapeDtypeStruct((TOK, EXTRA), BF16)),
+        in_specs=[VMEM] * 4,
+        out_specs=(HBM, VMEM),
+        scratch_shapes=[pltpu.VMEM((TOK, D), BF16), SEMS, SEMS, pltpu.SemaphoreType.DMA],
         compiler_params=params(0, 60),
-        cost_estimate=cost(1 << 22, 100 * MIB),
+        cost_estimate=cost(1 << 10, MIB),
         name="gather_tokens",
-    )(rows, attn_gain[None], routes[0], route_weights[0], expert_gate[0], expert_up[0], expert_down[0])
-
-    moe_shard, attn_weights = lax.optimization_barrier((moe_shard, attn_weights))
-    moe_weights = lax.all_gather(moe_shard, "dp", axis=0)
+    )(rows, attn_gain[None], routes[0].T, route_weights[0].T)
+
     cosine, sine = rope_tables()
-
     residual, everyone = pl.pallas_call(
         attend,
         out_shape=(
@@ -499,21 +580,29 @@
         out_specs=(VMEM, HBM),
         scratch_shapes=[
             pltpu.VMEM((16, TOK, D), BF16),
-            pltpu.VMEM((16, 768, 256), BF16),
+            pltpu.VMEM((16, 512, 256), BF16),
+            pltpu.VMEM((2, 8, 4, 256, 256), BF16),
             pltpu.VMEM((2, SEQ, HD), BF16),
             pltpu.VMEM((SEQ, HD), BF16),
             pltpu.VMEM((SEQ, HD), BF16),
-            pltpu.VMEM((16, TOK, 256), BF16),
+            pltpu.VMEM((4, 4, TOK, 256), BF16),
+            pltpu.VMEM((2, 4, TOK, 1024), BF16),
             pltpu.VMEM((TOK, D + EXTRA), BF16),
-            *RING,
+            pltpu.VMEM((2, 4, TOK, 2048), BF16),
+            pltpu.VMEM((2, 1, 2, HALF, 2048), BF16),
+            pltpu.VMEM((2, 1, 2, TOK, 2048), BF16),
+            pltpu.SemaphoreType.DMA((16,)),
+            pltpu.SemaphoreType.DMA((16,)),
+            pltpu.SemaphoreType.DMA((6,)),
+            pltpu.SemaphoreType.DMA((6,)),
             SEMS,
             SEMS,
             SEMS,
             SEMS,
-            pltpu.SemaphoreType.DMA((2,)),
+            pltpu.SemaphoreType.DMA((7,)),
         ],
         compiler_params=params(1, 56),
-        cost_estimate=cost(8 << 30, 150 * MIB),
+        cost_estimate=cost(1 << 10, MIB),
         name="attention",
     )(gathered, attn_weights, rows, cosine, sine, moe_gain[None], extra)
 

time: 251 us -> 238 us (0.948)
  Pallas kernels: 228 us -> 204 us
  waiting for transfers between devices: 0.08 us -> 18.2 us
  local copies, waits for them, and re-layouts: 5.51 us -> 1.87 us
    pallas_call x1, Pallas kernels: 113 us -> 86.7 us  [local(): pl.pallas_call(attend, out_shape=(jax.ShapeDtypeStruct((TOK, D), F32), ja...]
    all_gather x1, waiting for transfers between devices: 0.02 us -> 17.4 us  [local(): moe_weights = lax.all_gather(moe_shard, 'dp', axis=0)]
    unnamed x3 -> x1, local copies, waits for them, and re-layouts: 4.63 us -> 1.87 us
    pallas_call x0 -> x1, Pallas kernels: none -> 2.58 us  [local(): pl.pallas_call(pack_kernel, out_shape=(jax.ShapeDtypeStruct((768, 256), B...]
  transfers between devices with their start and end apart: 2 -> 2, of which waited for: 0 -> 1; matrix products, arithmetic and copies ran while one was open for 1% -> 0% of each run, Pallas kernels for 66% -> 58%
where the time goes in v2:
time: 238 us; the launch traced here: 237 us
  Pallas kernels  204 us (86%)
  waiting for transfers between devices  18.2 us (8%)
  between operations  13.4 us (6%)
    pallas_call x1, Pallas kernels, local(): pl.pallas_call(attend, out_shape=(jax.ShapeDtypeStruct((TOK, D), F32), ja...  86.7 us
    pallas_call x1, Pallas kernels, local(): pl.pallas_call(experts, out_shape=jax.ShapeDtypeStruct((TOK, D), BF16), i...  63.2 us
    pallas_call x1, Pallas kernels, local(): pl.pallas_call(gather_kernel, out_shape=(jax.ShapeDtypeStruct((16, TOK, D...  51.2 us
    all_gather x1, waiting for transfers between devices, local(): moe_weights = lax.all_gather(moe_shard, 'dp', axis=0)  17.4 us
  transfers between devices with their start and end apart: 2, of which 1 were waited for; matrix products, arithmetic and copies ran while one was open for 0% of the time, Pallas kernels for 58%

profile of v2, /device:TPU:1, one launch (start us, length us, event | category | flops | bytes accessed | tf_op | source)
XLA Modules:
  0.0 237.3 jit_solution(14810960931216370698)
XLA Ops:
  6.5 0.0 all-gather.5.cloned.1.call-start
  6.5 2.6 %pack_weights.1 = (bf16[768,256]{1,0:T(8,128)(2,1)}, bf16[2304,256]{1,0:T(8,128)(2,1)}) custom-call(bf16[256,768]{1,0:T(8,128)(2,1)} %bitcast.19, bf16[256,768]{1,0:T(8,128)(2,1)} %bitcast.20, bf16[48,4096]{1,0:T(8,128)(2,1)} %bitcast.21, bf16[256,256]{1,0:T(8,128)(2,1)} %w_query.1, bf16[256,256]{1,0:T(8,128)(2,1)} %w_key.1, bf16[256,256]{1,0:T(8,128)(2,1)} %w_value.1, ...), custom_call_target="tpu_custom_call" | custom-call | flops 1024 | bytes 4194304 | tf_op jit(solution)/shard_map/pack_weights/pallas_call | solution.py:549
  9.1 0.0 all-gather.5.cloned.1.call-update
  9.1 0.0 all-gather.7.cloned.1.call-start
  9.2 0.7 all-gather.7.cloned.1.call-update
  9.9 51.2 %gather_tokens.1 = (bf16[16,64,4096]{2,1,0:T(8,128)(2,1)}, bf16[64,128]{1,0:T(8,128)(2,1)}) custom-call(bf16[64,4096]{1,0:T(8,128)(2,1)} %bitcast.16, f32[1,4096]{1,0:T(1,128)} %bitcast.22, s32[8,64]{1,0:T(8,128)} %bitcast.24, f32[8,64]{1,0:T(8,128)} %bitcast.25), custom_call_target="tpu_custom_call" | custom-call | flops 1024 | bytes 1048576 | tf_op jit(solution)/shard_map/gather_tokens/pallas_call | solution.py:561
  61.1 0.0 all-gather.5.cloned.1.call-done
  61.2 86.7 %attention.1 = (f32[64,4096]{1,0:T(8,128)}, bf16[4,2,4,32,4224]{4,3,2,1,0:T(8,128)(2,1)}) custom-call(bf16[16,64,4096]{2,1,0:T(8,128)(2,1)} %get-tuple-element.11.gathered, bf16[16,768,256]{2,1,0:T(8,128)(2,1)} %bitcast.15, bf16[64,4096]{1,0:T(8,128)(2,1)} %bitcast.17, f32[1024,128]{1,0:T(8,128)} %constant.4.clone.cosine, f32[1024,128]{1,0:T(8,128)} %constant.5.clone.sine, ...), custom_call_target="tpu_custom_call" | custom-call | flops 1024 | bytes 1048576 | tf_op jit(solution)/shard_map/attention/pallas_call | solution.py:573
  147.9 17.4 %all-gather.7.cloned.1.call-done = bf16[36864,256]{1,0:T(8,128)(2,1)} async-done(((bf16[2304,256]{1,0:T(8,128)(2,1)}), bf16[36864,256]{1,0:T(8,128)(2,1)}) %all-gather.7.cloned.1.call-update) | async-done | bytes 18874384 | tf_op jit(solution)/shard_map/all_gather | solution.py:559
  165.3 63.2 %experts.1 = bf16[64,4096]{1,0:T(8,128)(2,1)} custom-call(bf16[4,2,4,32,4224]{4,3,2,1,0:T(8,128)(2,1)} %get-tuple-element.14.everyone, bf16[16,2304,256]{2,1,0:T(8,128)(2,1)} %bitcast.26, f32[64,4096]{1,0:T(8,128)} %get-tuple-element.16.residual), custom_call_target="tpu_custom_call" | custom-call | flops 21474836480 | bytes 209715200 | tf_op jit(solution)/shard_map/experts/pallas_call | solution.py:609
  228.6 1.9 copy.16
Async XLA Ops:
  6.5 54.6 %all-gather.5.cloned.1.call-start = ((), (), s32[]{:S(2)}) async-start(), calls=%async_computation | async-start | bytes 6684672 | tf_op jit(solution)/shard_map/all_gather | solution.py:558
  9.1 156.2 %all-gather.7.cloned.1.call-start = ((), (), s32[]{:S(2)}) async-start(), calls=%async_computation.1 | async-start | bytes 20054016 | tf_op jit(solution)/shard_map/all_gather | solution.py:559
Sparse Core Ops, SparseCore 0:
  9.3 50.2 all-gather.4
  61.4 103.9 all-gather.6

commit v3 on v2

--- a/solution.py
+++ b/solution.py
@@ -199,11 +199,46 @@
         return self.arrived(half, 0) + self.y[half, self.spots[half][0]].astype(F32)
 
 
+class Column:
+    def __init__(self, mine, w_ref, sends, recvs):
+        index = lax.axis_index("dp")
+        self.mine, self.w, self.sends, self.recvs = mine, w_ref, sends, recvs
+        self.level, self.core = index // 2, index % 2
+        self.other = {"dp": self.level * 2 + 1 - self.core}
+        self.next = [{"dp": (self.level + step) % 8 * 2 + self.core} for step in (1, 7)]
+        self.copies = {}
+
+    def send(self, slot, step, device, way=None):
+        start, rows = (0, 768) if way is None else (way * 384, 384)
+        place = self.w.at[(self.level + step) % 8 * 2 + self.core, pl.ds(start, rows)]
+        source = place if step else self.mine
+        self.copies[slot] = remote(source, place, self.sends, self.recvs, slot, device)
+
+    def start(self):
+        for way in (0, 1):
+            self.send(way * 4, 0, self.next[way])
+        self.send(8, 0, self.other)
+
+    def step(self, t):
+        for way in (0, 1):
+            self.copies[way * 4 + t - 1].wait_recv()
+            here = t if way else 8 - t
+            if t < 4:
+                self.send(way * 4 + t, here, self.next[way], way if t == 3 else None)
+            self.send(8 + way * 4 + t, here, self.other, way if t == 4 else None)
+
+    def finish(self):
+        for slot in range(8, 17):
+            self.copies[slot].wait_recv()
+        for copy in self.copies.values():
+            copy.wait_send()
+
+
 def normalized(values, gain):
     return values * lax.rsqrt(jnp.mean(values * values, axis=-1, keepdims=True) + 1e-06) * gain
 
 
-def pack_kernel(gate, up, down, w_query, w_key, w_value, w_out, attn_shard, moe_shard):
+def pack_kernel(gate, up, down, w_query, w_key, w_value, w_out, attn_shard, moe_shard, down_shard):
     key_cols = pl.ds(pl.multiple_of(lax.axis_index("expert") // 8 * HD, HD), HD)
     attn_shard[0:256] = w_query[...]
     attn_shard[256:512, 0:HD] = w_key[:, key_cols]
@@ -214,7 +249,7 @@
         moe_shard[cols] = gate[:, cols]
         moe_shard[FF + c * 256 : FF + c * 256 + 256] = up[:, cols]
     for c in range(16):
-        moe_shard[2 * FF + c * 48 : 2 * FF + c * 48 + 48] = down[:, c * 256 : c * 256 + 256]
+        down_shard[c * 48 : c * 48 + 48] = down[:, c * 256 : c * 256 + 256]
 
 
 def gather_kernel(
@@ -298,10 +333,10 @@
 
 
 def attend(
-    gathered, weights, tokens, cosine, sine, gain, extra,
-    residual, everyone,
+    gathered, weights, tokens, cosine, sine, gain, extra, down_shard,
+    residual, everyone, down_all,
     x, w, wo, queries, keys, values, mixed, mx, moe_in, y, small, large,
-    wo_sends, wo_recvs, mx_sends, mx_recvs, sends, recvs, out_sends, out_recvs, local,
+    wo_sends, wo_recvs, mx_sends, mx_recvs, sends, recvs, out_sends, out_recvs, z_sends, z_recvs, local,
 ):
     spots = place()
     load_w = pltpu.make_async_copy(weights.at[:, pl.ds(0, 512)], w, local.at[0])
@@ -319,8 +354,12 @@
         loads[-1].start()
     share = Share(spots, weights, wo, wo_sends, wo_recvs)
     across = [device(f, turn(s, 2)) for f, s, device in spots]
-    meet(around(spots) + across + [share.other])
+    column = Column(down_shard, down_all, z_sends, z_recvs)
+    own_down = pltpu.make_async_copy(down_shard, down_all.at[lax.axis_index("dp")], local.at[7])
+    own_down.start()
+    meet(around(spots) + across + column.next + [column.other])
     share.start()
+    column.start()
     load_w.wait()
 
     def rope(part, rows):
@@ -354,6 +393,7 @@
     for i in range(4):
         project(i)
     share.forward()
+    column.step(1)
     for i in range(4):
         attention(i)
 
@@ -382,15 +422,10 @@
 
     fold = Fold(spots, y, small, large, None, sends, recvs, HALF)
     for half in (0, 1):
-
-        @pl.loop(0, 2)
-        def _(group):
-            left = mx[half].reshape(256, 1024)
-            for c in range(4):
-                right = wo[half, group * 4 + c].reshape(1024, 256)
-                part = jnp.dot(left, right, preferred_element_type=F32)
-                cols = pl.ds(pl.multiple_of(group * 1024 + c * 256, 256), 256)
-                y[half, :, :, cols] = part.astype(BF16).reshape(4, TOK, 256)
+        left = mx[half].reshape(256, 1024)
+        for c in range(8):
+            part = jnp.dot(left, wo[half, c].reshape(1024, 256), preferred_element_type=F32)
+            y[half, :, :, c * 256 : c * 256 + 256] = part.astype(BF16).reshape(4, TOK, 256)
 
     fold.start(0)
     for copy in swaps:
@@ -413,15 +448,28 @@
         keeps.append(pltpu.make_async_copy(gather.own(half), block(0, half, s, 0, HALF), local.at[half]))
         keeps[-1].start()
     fold.drain()
-    gather.rest()
+    gather.second_hop()
+    gather.forward(0)
+    column.step(2)
+    gather.last_hop()
+    gather.forward(1)
+    gather.forward(2)
+    column.step(3)
+    gather.forward(3)
+    for r in range(4):
+        gather.finish(r)
+    column.step(4)
+    gather.drain()
     for keep in keeps:
         keep.wait()
+    column.finish()
+    own_down.wait()
 
 
 def experts(
-    everyone, weights, residual,
+    everyone, weights, down_all, residual,
     out,
-    g, w, act, y, small, large, z, sends, recvs, load_g, load_w, load_down,
+    g, w, wd, act, y, small, large, z, sends, recvs, load_g, load_w, load_down,
 ):
     spots = place()
     rows_of = [pltpu.make_async_copy(everyone.at[r], g.at[r], load_g.at[r]) for r in range(4)]
@@ -430,14 +478,13 @@
         part = (c // 2 + c % 2 * 3) * 256
         view = pl.ds(part, 256)
         feeds.append(pltpu.make_async_copy(weights.at[:, view], w.at[:, view], load_w.at[c]))
-    view = pl.ds(2 * FF, FF)
-    downs = pltpu.make_async_copy(weights.at[:, view], w.at[:, view], load_down)
+    downs = pltpu.make_async_copy(down_all, wd, load_down)
     rows_of[3].start()
     for copy in feeds:
         copy.start()
+    downs.start()
     for r in (2, 1, 0):
         rows_of[r].start()
-    downs.start()
     meet(around(spots))
     scatter = Scatter(spots, y, small, large, z, sends, recvs)
     index = lax.axis_index("expert")
@@ -463,14 +510,10 @@
         chosen = (lanes == index) | (lanes == index + 16)
         share = jnp.sum(jnp.where(chosen, table, 0.0), axis=-1, keepdims=True)
 
-        @pl.loop(0, 4)
-        def _(group):
-            for c in range(4):
-                n = group * 4 + c
-                right = w[:, pl.ds(pl.multiple_of(2 * FF + n * 48, 16), 48)].reshape(FF, 256)
-                part = jnp.dot(act[...], right, preferred_element_type=F32) * share
-                cols = pl.ds(pl.multiple_of(n * 256, 256), 256)
-                y[r, :, :, :, cols] = part.astype(BF16).reshape(2, 4, HALF, 256)
+        for n in range(16):
+            right = wd[:, n * 48 : n * 48 + 48].reshape(FF, 256)
+            part = jnp.dot(act[...], right, preferred_element_type=F32) * share
+            y[r, :, :, :, n * 256 : n * 256 + 256] = part.astype(BF16).reshape(2, 4, HALF, 256)
 
     feed(3)
     downs.wait()
@@ -546,11 +589,15 @@
     route_weights,
 ):
     rows = tokens[0]
-    attn_shard, moe_shard = pl.pallas_call(
+    attn_shard, moe_shard, down_shard = pl.pallas_call(
         pack_kernel,
-        out_shape=(jax.ShapeDtypeStruct((768, 256), BF16), jax.ShapeDtypeStruct((2304, 256), BF16)),
+        out_shape=(
+            jax.ShapeDtypeStruct((768, 256), BF16),
+            jax.ShapeDtypeStruct((1536, 256), BF16),
+            jax.ShapeDtypeStruct((768, 256), BF16),
+        ),
         in_specs=[VMEM] * 7,
-        out_specs=(VMEM, VMEM),
+        out_specs=(VMEM, VMEM, VMEM),
         compiler_params=pltpu.CompilerParams(vmem_limit_bytes=60 * MIB),
         cost_estimate=cost(1 << 10, 4 * MIB),
         name="pack_weights",
@@ -570,14 +617,15 @@
     )(rows, attn_gain[None], routes[0].T, route_weights[0].T)
 
     cosine, sine = rope_tables()
-    residual, everyone = pl.pallas_call(
+    residual, everyone, down_all = pl.pallas_call(
         attend,
         out_shape=(
             jax.ShapeDtypeStruct((TOK, D), F32),
             jax.ShapeDtypeStruct((4, 2, 4, HALF, D + EXTRA), BF16),
+            jax.ShapeDtypeStruct((16, 768, 256), BF16),
         ),
-        in_specs=[ANY, ANY, VMEM, VMEM, VMEM, VMEM, VMEM],
-        out_specs=(VMEM, HBM),
+        in_specs=[ANY, ANY, VMEM, VMEM, VMEM, VMEM, VMEM, ANY],
+        out_specs=(VMEM, HBM, HBM),
         scratch_shapes=[
             pltpu.VMEM((16, TOK, D), BF16),
             pltpu.VMEM((16, 512, 256), BF16),
@@ -599,21 +647,24 @@
             SEMS,
             SEMS,
             SEMS,
-            pltpu.SemaphoreType.DMA((7,)),
+            pltpu.SemaphoreType.DMA((17,)),
+            pltpu.SemaphoreType.DMA((17,)),
+            pltpu.SemaphoreType.DMA((8,)),
         ],
         compiler_params=params(1, 56),
         cost_estimate=cost(1 << 10, MIB),
         name="attention",
-    )(gathered, attn_weights, rows, cosine, sine, moe_gain[None], extra)
+    )(gathered, attn_weights, rows, cosine, sine, moe_gain[None], extra, down_shard)
 
     layer_out = pl.pallas_call(
         experts,
         out_shape=jax.ShapeDtypeStruct((TOK, D), BF16),
-        in_specs=[ANY, ANY, VMEM],
+        in_specs=[ANY, ANY, ANY, VMEM],
         out_specs=VMEM,
         scratch_shapes=[
             pltpu.VMEM((4, 2, 4, HALF, D + EXTRA), BF16),
-            pltpu.VMEM((16, 2304, 256), BF16),
+            pltpu.VMEM((16, 1536, 256), BF16),
+            pltpu.VMEM((16, 768, 256), BF16),
             pltpu.VMEM((256, FF), BF16),
             *RING,
             SEMS,
@@ -625,7 +676,7 @@
         compiler_params=params(2, 60),
         cost_estimate=cost(20 << 30, 200 * MIB),
         name="experts",
-    )(everyone, moe_weights, residual)
+    )(everyone, moe_weights, down_all, residual)
     return layer_out[None]
 
 

time: 238 us -> 230 us (0.966)
  waiting for transfers between devices: 18.2 us -> 2.99 us
  Pallas kernels: 204 us -> 212 us
    all_gather x1, waiting for transfers between devices: 17.4 us -> 2.26 us  [local(): moe_weights = lax.all_gather(moe_shard, 'dp', axis=0)]
    pallas_call x1, Pallas kernels: 86.7 us -> 98.3 us  [local(): pl.pallas_call(attend, out_shape=(jax.ShapeDtypeStruct((TOK, D), F32), ja...]
    pallas_call x1, Pallas kernels: 63.2 us -> 59.5 us  [local(): pl.pallas_call(experts, out_shape=jax.ShapeDtypeStruct((TOK, D), BF16), i...]
  transfers between devices with their start and end apart: 2 -> 2, of which waited for: 1 -> 1; matrix products, arithmetic and copies ran while one was open for 0% -> 0% of each run, Pallas kernels for 58% -> 65%
where the time goes in v3:
time: 230 us
  Pallas kernels  212 us (92%)
  between operations  13.4 us (6%)
  waiting for transfers between devices  2.99 us (1%)
    pallas_call x1, Pallas kernels, local(): pl.pallas_call(attend, out_shape=(jax.ShapeDtypeStruct((TOK, D), F32), ja...  98.3 us
    pallas_call x1, Pallas kernels, local(): pl.pallas_call(experts, out_shape=jax.ShapeDtypeStruct((TOK, D), BF16), i...  59.5 us
    pallas_call x1, Pallas kernels, local(): pl.pallas_call(gather_kernel, out_shape=(jax.ShapeDtypeStruct((16, TOK, D...  51.2 us
  transfers between devices with their start and end apart: 2, of which 1 were waited for; matrix products, arithmetic and copies ran while one was open for 0% of the time, Pallas kernels for 65%

profile of v3, /device:TPU:1, one launch (start us, length us, event | category | flops | bytes accessed | tf_op | source)
XLA Modules:
  0.0 230.0 jit_solution(12732940906926337990)
XLA Ops:
  6.5 0.0 all-gather.5.cloned.1.call-start
  6.5 2.6 %pack_weights.1 = (bf16[768,256]{1,0:T(8,128)(2,1)}, bf16[1536,256]{1,0:T(8,128)(2,1)}, bf16[768,256]{1,0:T(8,128)(2,1)}) custom-call(bf16[256,768]{1,0:T(8,128)(2,1)} %bitcast.19, bf16[256,768]{1,0:T(8,128)(2,1)} %bitcast.20, bf16[48,4096]{1,0:T(8,128)(2,1)} %bitcast.21, bf16[256,256]{1,0:T(8,128)(2,1)} %w_query.1, bf16[256,256]{1,0:T(8,128)(2,1)} %w_key.1, ...), custom_call_target="tpu_custom_call" | custom-call | flops 1024 | bytes 4194304 | tf_op jit(solution)/shard_map/pack_weights/pallas_call | solution.py:592
  9.1 0.0 all-gather.5.cloned.1.call-update
  9.2 0.0 all-gather.7.cloned.1.call-start
  9.2 0.7 all-gather.7.cloned.1.call-update
  9.9 51.2 %gather_tokens.1 = (bf16[16,64,4096]{2,1,0:T(8,128)(2,1)}, bf16[64,128]{1,0:T(8,128)(2,1)}) custom-call(bf16[64,4096]{1,0:T(8,128)(2,1)} %bitcast.16, f32[1,4096]{1,0:T(1,128)} %bitcast.22, s32[8,64]{1,0:T(8,128)} %bitcast.24, f32[8,64]{1,0:T(8,128)} %bitcast.25), custom_call_target="tpu_custom_call" | custom-call | flops 1024 | bytes 1048576 | tf_op jit(solution)/shard_map/gather_tokens/pallas_call | solution.py:608
  61.2 0.0 all-gather.5.cloned.1.call-done
  61.2 98.3 %attention.1 = (f32[64,4096]{1,0:T(8,128)}, bf16[4,2,4,32,4224]{4,3,2,1,0:T(8,128)(2,1)}, bf16[16,768,256]{2,1,0:T(8,128)(2,1)}) custom-call(bf16[16,64,4096]{2,1,0:T(8,128)(2,1)} %get-tuple-element.13.gathered, bf16[16,768,256]{2,1,0:T(8,128)(2,1)} %bitcast.15, bf16[64,4096]{1,0:T(8,128)(2,1)} %bitcast.17, f32[1024,128]{1,0:T(8,128)} %constant.4.clone.cosine, ...), custom_call_target="tpu_custom_call" | custom-call | flops 1024 | bytes 1048576 | tf_op jit(solution)/shard_map/attention/pallas_call | solution.py:620
  159.5 2.3 all-gather.7.cloned.1.call-done
  161.7 59.5 %experts.1 = bf16[64,4096]{1,0:T(8,128)(2,1)} custom-call(bf16[4,2,4,32,4224]{4,3,2,1,0:T(8,128)(2,1)} %get-tuple-element.17.everyone, bf16[16,1536,256]{2,1,0:T(8,128)(2,1)} %bitcast.26, bf16[16,768,256]{2,1,0:T(8,128)(2,1)} %get-tuple-element.19.down_all, f32[64,4096]{1,0:T(8,128)} %get-tuple-element.20.residual), custom_call_target="tpu_custom_call" | custom-call | flops 21474836480 | bytes 209715200 | tf_op jit(solution)/shard_map/experts/pallas_call | solution.py:659
  221.3 1.9 copy.16
Async XLA Ops:
  6.5 54.7 %all-gather.5.cloned.1.call-start = ((), (), s32[]{:S(2)}) async-start(), calls=%async_computation | async-start | bytes 6684672 | tf_op jit(solution)/shard_map/all_gather | solution.py:605
  9.2 152.6 %all-gather.7.cloned.1.call-start = ((), (), s32[]{:S(2)}) async-start(), calls=%async_computation.1 | async-start | bytes 13369344 | tf_op jit(solution)/shard_map/all_gather | solution.py:606
Sparse Core Ops, SparseCore 0:
  9.3 50.2 all-gather.4
  61.4 100.2 all-gather.6

commit v4 on v3

--- a/solution.py
+++ b/solution.py
@@ -16,6 +16,8 @@
 HALF = 32
 SEQ = 1024
 EXTRA = 128
+EARLY = 1056
+LATE = 480
 MESH = pl.DeviceIdType.MESH
 F32 = jnp.float32
 BF16 = jnp.bfloat16
@@ -94,7 +96,6 @@
                 source = self.block(1 + lane, half, s, lane * 16, 16)
                 target = source if self.absolute else self.block(3, half, s, lane * 16, 16)
                 self.send(half, 4, 2 + lane, source, target, device(turn(f, step), s))
-                self.spread(1 + lane, (half,))
 
     def last_hop(self):
         for half in (0, 1):
@@ -114,14 +115,21 @@
             for lane in (2, 3):
                 self.copies[half, r, lane].wait_recv()
 
-    def rest(self):
+    def rest(self, between):
         self.second_hop()
         self.forward(0)
+        self.spread(1)
         self.last_hop()
-        for r in (1, 2, 3):
-            self.forward(r)
+        self.spread(2)
+        between[0]()
+        self.forward(1)
+        between[1]()
+        self.forward(3)
+        self.forward(2)
+        between[2]()
         for r in range(4):
             self.finish(r)
+        between[3]()
         self.drain()
 
     def drain(self):
@@ -153,8 +161,8 @@
             lambda step: device(turn(f, step), s),
         )
 
-    def start(self, group):
-        for half in (0, 1):
+    def start(self, group, halves=(0, 1)):
+        for half in halves:
             block, device = self.parts(half, group)
             for lane, step in ((0, 1), (1, 3)):
                 self.send(
@@ -200,16 +208,16 @@
 
 
 class Column:
-    def __init__(self, mine, w_ref, sends, recvs):
+    def __init__(self, mine, w_ref, rows, sends, recvs):
         index = lax.axis_index("dp")
-        self.mine, self.w, self.sends, self.recvs = mine, w_ref, sends, recvs
+        self.mine, self.w, self.rows, self.sends, self.recvs = mine, w_ref, rows, sends, recvs
         self.level, self.core = index // 2, index % 2
         self.other = {"dp": self.level * 2 + 1 - self.core}
         self.next = [{"dp": (self.level + step) % 8 * 2 + self.core} for step in (1, 7)]
         self.copies = {}
 
     def send(self, slot, step, device, way=None):
-        start, rows = (0, 768) if way is None else (way * 384, 384)
+        start, rows = (0, self.rows) if way is None else (way * self.rows // 2, self.rows // 2)
         place = self.w.at[(self.level + step) % 8 * 2 + self.core, pl.ds(start, rows)]
         source = place if step else self.mine
         self.copies[slot] = remote(source, place, self.sends, self.recvs, slot, device)
@@ -238,31 +246,34 @@
     return values * lax.rsqrt(jnp.mean(values * values, axis=-1, keepdims=True) + 1e-06) * gain
 
 
-def pack_kernel(gate, up, down, w_query, w_key, w_value, w_out, attn_shard, moe_shard, down_shard):
-    key_cols = pl.ds(pl.multiple_of(lax.axis_index("expert") // 8 * HD, HD), HD)
-    attn_shard[0:256] = w_query[...]
-    attn_shard[256:512, 0:HD] = w_key[:, key_cols]
-    attn_shard[256:512, HD:] = w_value[:, key_cols]
-    attn_shard[512:768] = w_out[...]
-    for c in range(3):
-        cols = slice(c * 256, c * 256 + 256)
-        moe_shard[cols] = gate[:, cols]
-        moe_shard[FF + c * 256 : FF + c * 256 + 256] = up[:, cols]
-    for c in range(16):
-        down_shard[c * 48 : c * 48 + 48] = down[:, c * 256 : c * 256 + 256]
-
-
 def gather_kernel(
-    tokens, gain, routes, weights,
-    out, extra,
-    own, sends, recvs, local,
+    tokens, gain, routes, weights, gate, up, down, w_query, w_key, w_value, w_out,
+    out, extra, w_all, feed_shard, down_shard,
+    own, parts, wide, tall, shard, sends, recvs, w_sends, w_recvs, local,
 ):
     spots = place()
     index = lax.axis_index("expert")
+    loads = [
+        pltpu.make_async_copy(source, target, local.at[i])
+        for i, (source, target) in enumerate(
+            (
+                (w_query, parts.at[0]),
+                (w_key, parts.at[1]),
+                (w_value, parts.at[2]),
+                (w_out, parts.at[3]),
+                (down, tall),
+                (gate, wide.at[0]),
+                (up, wide.at[1]),
+            )
+        )
+    ]
+    for copy in loads:
+        copy.start()
     own[...] = normalized(tokens[...].astype(F32), gain[...]).astype(BF16)
-    keep = pltpu.make_async_copy(own, out.at[index], local)
+    keep = pltpu.make_async_copy(own, out.at[index], local.at[7])
     keep.start()
-    meet(around(spots))
+    column = Column(shard, w_all, EARLY, w_sends, w_recvs)
+    meet(around(spots) + column.next + [column.other])
 
     def block(r, half, second, start, rows):
         f, _, device = spots[half]
@@ -270,6 +281,23 @@
 
     gather = Gather(spots, block, sends, recvs, lambda half: own.at[pl.ds(half * HALF, HALF)], True)
     gather.first_hop()
+
+    for copy in loads:
+        copy.wait()
+    key_cols = pl.ds(pl.multiple_of(index // 8 * HD, HD), HD)
+    shard[0:256] = parts[0]
+    shard[256:512, 0:HD] = parts[1, :, key_cols]
+    shard[256:512, HD:] = parts[2, :, key_cols]
+    shard[512:768] = parts[3]
+    for c in range(6):
+        shard[768 + c * 48 : 816 + c * 48] = tall[:, c * 256 : c * 256 + 256]
+    mine = pltpu.make_async_copy(shard, w_all.at[lax.axis_index("dp")], local.at[0])
+    mine.start()
+    column.start()
+    for c in range(6, 16):
+        down_shard[c * 48 - 288 : c * 48 - 240] = tall[:, c * 256 : c * 256 + 256]
+    for c in range(6):
+        feed_shard[c * 256 : c * 256 + 256] = wide[c // 3, :, c % 3 * 256 : c % 3 * 256 + 256]
 
     share = weights[...] / jnp.sum(weights[...], axis=0, keepdims=True)
     high = share.astype(BF16).astype(F32)
@@ -282,8 +310,10 @@
         table += jnp.where(at_row == named + 16, low[k : k + 1], 0.0)
     extra[...] = table.T.astype(BF16)
 
-    gather.rest()
+    gather.rest([lambda t=t: column.step(t) for t in (1, 2, 3, 4)])
     keep.wait()
+    mine.wait()
+    column.finish()
 
 
 class Share:
@@ -354,7 +384,7 @@
         loads[-1].start()
     share = Share(spots, weights, wo, wo_sends, wo_recvs)
     across = [device(f, turn(s, 2)) for f, s, device in spots]
-    column = Column(down_shard, down_all, z_sends, z_recvs)
+    column = Column(down_shard, down_all, LATE, z_sends, z_recvs)
     own_down = pltpu.make_async_copy(down_shard, down_all.at[lax.axis_index("dp")], local.at[7])
     own_down.start()
     meet(around(spots) + across + column.next + [column.other])
@@ -426,11 +456,11 @@
         for c in range(8):
             part = jnp.dot(left, wo[half, c].reshape(1024, 256), preferred_element_type=F32)
             y[half, :, :, c * 256 : c * 256 + 256] = part.astype(BF16).reshape(4, TOK, 256)
-
-    fold.start(0)
+        fold.start(0, (half,))
     for copy in swaps:
         copy.wait_send()
     share.drain()
+    column.step(2)
     fold.middle(0)
     for half in (0, 1):
         cols = slice(half * 2048, (half + 1) * 2048)
@@ -448,18 +478,7 @@
         keeps.append(pltpu.make_async_copy(gather.own(half), block(0, half, s, 0, HALF), local.at[half]))
         keeps[-1].start()
     fold.drain()
-    gather.second_hop()
-    gather.forward(0)
-    column.step(2)
-    gather.last_hop()
-    gather.forward(1)
-    gather.forward(2)
-    column.step(3)
-    gather.forward(3)
-    for r in range(4):
-        gather.finish(r)
-    column.step(4)
-    gather.drain()
+    gather.rest([lambda: column.step(3), lambda: column.step(4), lambda: None, lambda: None])
     for keep in keeps:
         keep.wait()
     column.finish()
@@ -467,7 +486,7 @@
 
 
 def experts(
-    everyone, weights, down_all, residual,
+    everyone, weights, w_all, down_all, residual,
     out,
     g, w, wd, act, y, small, large, z, sends, recvs, load_g, load_w, load_down,
 ):
@@ -478,11 +497,15 @@
         part = (c // 2 + c % 2 * 3) * 256
         view = pl.ds(part, 256)
         feeds.append(pltpu.make_async_copy(weights.at[:, view], w.at[:, view], load_w.at[c]))
-    downs = pltpu.make_async_copy(down_all, wd, load_down)
+    downs = [
+        pltpu.make_async_copy(w_all.at[:, pl.ds(768, 288)], wd.at[:, pl.ds(0, 288)], load_down.at[0]),
+        pltpu.make_async_copy(down_all, wd.at[:, pl.ds(288, LATE)], load_down.at[1]),
+    ]
     rows_of[3].start()
     for copy in feeds:
         copy.start()
-    downs.start()
+    for copy in downs:
+        copy.start()
     for r in (2, 1, 0):
         rows_of[r].start()
     meet(around(spots))
@@ -516,7 +539,8 @@
             y[r, :, :, :, n * 256 : n * 256 + 256] = part.astype(BF16).reshape(2, 4, HALF, 256)
 
     feed(3)
-    downs.wait()
+    for copy in downs:
+        copy.wait()
     down(3)
     scatter.start(3)
     feed(2)
@@ -589,32 +613,37 @@
     route_weights,
 ):
     rows = tokens[0]
-    attn_shard, moe_shard, down_shard = pl.pallas_call(
-        pack_kernel,
+    gathered, extra, w_all, feed_shard, down_shard = pl.pallas_call(
+        gather_kernel,
         out_shape=(
-            jax.ShapeDtypeStruct((768, 256), BF16),
+            jax.ShapeDtypeStruct((16, TOK, D), BF16),
+            jax.ShapeDtypeStruct((TOK, EXTRA), BF16),
+            jax.ShapeDtypeStruct((16, EARLY, 256), BF16),
             jax.ShapeDtypeStruct((1536, 256), BF16),
-            jax.ShapeDtypeStruct((768, 256), BF16),
+            jax.ShapeDtypeStruct((LATE, 256), BF16),
         ),
-        in_specs=[VMEM] * 7,
-        out_specs=(VMEM, VMEM, VMEM),
-        compiler_params=pltpu.CompilerParams(vmem_limit_bytes=60 * MIB),
-        cost_estimate=cost(1 << 10, 4 * MIB),
-        name="pack_weights",
-    )(expert_gate[0], expert_up[0], expert_down[0], w_query, w_key, w_value, w_out)
-    attn_weights = lax.all_gather(attn_shard, "dp", axis=0)
-    moe_weights = lax.all_gather(moe_shard, "dp", axis=0)
-
-    gathered, extra = pl.pallas_call(
-        gather_kernel,
-        out_shape=(jax.ShapeDtypeStruct((16, TOK, D), BF16), jax.ShapeDtypeStruct((TOK, EXTRA), BF16)),
-        in_specs=[VMEM] * 4,
-        out_specs=(HBM, VMEM),
-        scratch_shapes=[pltpu.VMEM((TOK, D), BF16), SEMS, SEMS, pltpu.SemaphoreType.DMA],
+        in_specs=[VMEM] * 4 + [ANY] * 7,
+        out_specs=(HBM, VMEM, HBM, VMEM, VMEM),
+        scratch_shapes=[
+            pltpu.VMEM((TOK, D), BF16),
+            pltpu.VMEM((4, 256, 256), BF16),
+            pltpu.VMEM((2, 256, FF), BF16),
+            pltpu.VMEM((48, D), BF16),
+            pltpu.VMEM((EARLY, 256), BF16),
+            SEMS,
+            SEMS,
+            pltpu.SemaphoreType.DMA((17,)),
+            pltpu.SemaphoreType.DMA((17,)),
+            pltpu.SemaphoreType.DMA((8,)),
+        ],
         compiler_params=params(0, 60),
         cost_estimate=cost(1 << 10, MIB),
         name="gather_tokens",
-    )(rows, attn_gain[None], routes[0].T, route_weights[0].T)
+    )(
+        rows, attn_gain[None], routes[0].T, route_weights[0].T,
+        expert_gate[0], expert_up[0], expert_down[0], w_query, w_key, w_value, w_out,
+    )
+    feed_weights = lax.all_gather(feed_shard, "dp", axis=0)
 
     cosine, sine = rope_tables()
     residual, everyone, down_all = pl.pallas_call(
@@ -622,7 +651,7 @@
         out_shape=(
             jax.ShapeDtypeStruct((TOK, D), F32),
             jax.ShapeDtypeStruct((4, 2, 4, HALF, D + EXTRA), BF16),
-            jax.ShapeDtypeStruct((16, 768, 256), BF16),
+            jax.ShapeDtypeStruct((16, LATE, 256), BF16),
         ),
         in_specs=[ANY, ANY, VMEM, VMEM, VMEM, VMEM, VMEM, ANY],
         out_specs=(VMEM, HBM, HBM),
@@ -654,12 +683,12 @@
         compiler_params=params(1, 56),
         cost_estimate=cost(1 << 10, MIB),
         name="attention",
-    )(gathered, attn_weights, rows, cosine, sine, moe_gain[None], extra, down_shard)
+    )(gathered, w_all, rows, cosine, sine, moe_gain[None], extra, down_shard)
 
     layer_out = pl.pallas_call(
         experts,
         out_shape=jax.ShapeDtypeStruct((TOK, D), BF16),
-        in_specs=[ANY, ANY, ANY, VMEM],
+        in_specs=[ANY, ANY, ANY, ANY, VMEM],
         out_specs=VMEM,
         scratch_shapes=[
             pltpu.VMEM((4, 2, 4, HALF, D + EXTRA), BF16),
@@ -671,12 +700,12 @@
             SEMS,
             pltpu.SemaphoreType.DMA((4,)),
             pltpu.SemaphoreType.DMA((6,)),
-            pltpu.SemaphoreType.DMA,
+            pltpu.SemaphoreType.DMA((2,)),
         ],
         compiler_params=params(2, 60),
         cost_estimate=cost(20 << 30, 200 * MIB),
         name="experts",
-    )(everyone, moe_weights, down_all, residual)
+    )(everyone, feed_weights, w_all, down_all, residual)
     return layer_out[None]
 
 

time: 230 us -> 228 us (level)
  waiting for transfers between devices: 2.99 us -> 0.04 us
    pallas_call x1, Pallas kernels: 51.2 us -> 63.7 us  [local(): pl.pallas_call(gather_kernel, out_shape=(jax.ShapeDtypeStruct((16, TOK, D...]
    pallas_call x1, Pallas kernels: 98.3 us -> 90.1 us  [local(): pl.pallas_call(attend, out_shape=(jax.ShapeDtypeStruct((TOK, D), F32), ja...]
    pallas_call x1, Pallas kernels: 59.5 us -> 56.9 us  [local(): pl.pallas_call(experts, out_shape=jax.ShapeDtypeStruct((TOK, D), BF16), i...]
    pallas_call x1 -> x0, Pallas kernels: 2.6 us -> none  [local(): pl.pallas_call(pack_kernel, out_shape=(jax.ShapeDtypeStruct((768, 256), B...]
  transfers between devices with their start and end apart: 2 -> 1, of which waited for: 1 -> 0; matrix products, arithmetic and copies ran while one was open for 0% -> 0% of each run, Pallas kernels for 65% -> 40%
where the time goes in v4:
time: 228 us; the launch traced here: 226 us
  Pallas kernels  211 us (93%)
  between operations  13.4 us (6%)
    pallas_call x1, Pallas kernels, local(): pl.pallas_call(attend, out_shape=(jax.ShapeDtypeStruct((TOK, D), F32), ja...  90.1 us
    pallas_call x1, Pallas kernels, local(): pl.pallas_call(gather_kernel, out_shape=(jax.ShapeDtypeStruct((16, TOK, D...  63.7 us
    pallas_call x1, Pallas kernels, local(): pl.pallas_call(experts, out_shape=jax.ShapeDtypeStruct((TOK, D), BF16), i...  56.9 us
  transfers between devices with their start and end apart: 1, of which 0 were waited for; matrix products, arithmetic and copies ran while one was open for 0% of the time, Pallas kernels for 40%

profile of v4, /device:TPU:1, one launch (start us, length us, event | category | flops | bytes accessed | tf_op | source)
XLA Modules:
  0.0 226.0 jit_solution(17545245449180358311)
XLA Ops:
  6.5 0.0 all-gather.3.cloned.1.call-start
  6.5 63.7 %gather_tokens.1 = (bf16[16,64,4096]{2,1,0:T(8,128)(2,1)}, bf16[64,128]{1,0:T(8,128)(2,1)}, bf16[16,1056,256]{2,1,0:T(8,128)(2,1)}, bf16[1536,256]{1,0:T(8,128)(2,1)}, bf16[480,256]{1,0:T(8,128)(2,1)}) custom-call(bf16[64,4096]{1,0:T(8,128)(2,1)} %bitcast.14, f32[1,4096]{1,0:T(1,128)} %bitcast.20, s32[8,64]{1,0:T(8,128)} %bitcast.22, f32[8,64]{1,0:T(8,128)} %bitcast.23, ...), custom_call_target="tpu_custom_call" | custom-call | flops 1024 | bytes 1048576 | tf_op jit(solution)/shard_map/gather_tokens/pallas_call | solution.py:616
  70.2 0.0 all-gather.3.cloned.1.call-update
  70.2 90.1 %attention.1 = (f32[64,4096]{1,0:T(8,128)}, bf16[4,2,4,32,4224]{4,3,2,1,0:T(8,128)(2,1)}, bf16[16,480,256]{2,1,0:T(8,128)(2,1)}) custom-call(bf16[16,64,4096]{2,1,0:T(8,128)(2,1)} %get-tuple-element.13.gathered, bf16[16,1056,256]{2,1,0:T(8,128)(2,1)} %get-tuple-element.14.weights.w_all, bf16[64,4096]{1,0:T(8,128)(2,1)} %bitcast.15, ...), custom_call_target="tpu_custom_call" | custom-call | flops 1024 | bytes 1048576 | tf_op jit(solution)/shard_map/attention/pallas_call | solution.py:649
  160.3 0.0 all-gather.3.cloned.1.call-done
  160.4 56.9 %experts.1 = bf16[64,4096]{1,0:T(8,128)(2,1)} custom-call(bf16[4,2,4,32,4224]{4,3,2,1,0:T(8,128)(2,1)} %get-tuple-element.17.everyone, bf16[16,1536,256]{2,1,0:T(8,128)(2,1)} %bitcast.24, bf16[16,1056,256]{2,1,0:T(8,128)(2,1)} %get-tuple-element.14.weights.w_all, bf16[16,480,256]{2,1,0:T(8,128)(2,1)} %get-tuple-element.19.down_all, ...), custom_call_target="tpu_custom_call" | custom-call | flops 21474836480 | bytes 209715200 | tf_op jit(solution)/shard_map/experts/pallas_call | solution.py:688
  217.3 1.9 copy.16
Async XLA Ops:
  6.5 153.8 %all-gather.3.cloned.1.call-start = ((), (), s32[]{:S(2)}) async-start(), calls=%async_computation | async-start | bytes 13369344 | tf_op jit(solution)/shard_map/all_gather | solution.py:646
Sparse Core Ops, SparseCore 0:
  70.4 85.3 all-gather.2

commit v5 on v3

--- a/solution.py
+++ b/solution.py
@@ -16,6 +16,8 @@
 HALF = 32
 SEQ = 1024
 EXTRA = 128
+EARLY = ((0, 512), (512, 256))
+LATE = ((0, 576), (576, 576), (1152, 576), (1728, 576))
 MESH = pl.DeviceIdType.MESH
 F32 = jnp.float32
 BF16 = jnp.bfloat16
@@ -94,7 +96,6 @@
                 source = self.block(1 + lane, half, s, lane * 16, 16)
                 target = source if self.absolute else self.block(3, half, s, lane * 16, 16)
                 self.send(half, 4, 2 + lane, source, target, device(turn(f, step), s))
-                self.spread(1 + lane, (half,))
 
     def last_hop(self):
         for half in (0, 1):
@@ -114,14 +115,23 @@
             for lane in (2, 3):
                 self.copies[half, r, lane].wait_recv()
 
-    def rest(self):
+    def rest(self, between):
         self.second_hop()
         self.forward(0)
+        between[0]()
+        self.spread(1)
         self.last_hop()
-        for r in (1, 2, 3):
-            self.forward(r)
+        self.spread(2)
+        between[1]()
+        self.forward(1)
+        between[2]()
+        self.forward(3)
+        between[3]()
+        self.forward(2)
+        between[4]()
         for r in range(4):
             self.finish(r)
+        between[5]()
         self.drain()
 
     def drain(self):
@@ -153,8 +163,8 @@
             lambda step: device(turn(f, step), s),
         )
 
-    def start(self, group):
-        for half in (0, 1):
+    def start(self, group, halves=(0, 1)):
+        for half in halves:
             block, device = self.parts(half, group)
             for lane, step in ((0, 1), (1, 3)):
                 self.send(
@@ -200,17 +210,17 @@
 
 
 class Column:
-    def __init__(self, mine, w_ref, sends, recvs):
+    def __init__(self, mine, w_ref, base, rows, sends, recvs):
         index = lax.axis_index("dp")
-        self.mine, self.w, self.sends, self.recvs = mine, w_ref, sends, recvs
+        self.mine, self.w, self.base, self.rows, self.sends, self.recvs = mine, w_ref, base, rows, sends, recvs
         self.level, self.core = index // 2, index % 2
         self.other = {"dp": self.level * 2 + 1 - self.core}
         self.next = [{"dp": (self.level + step) % 8 * 2 + self.core} for step in (1, 7)]
         self.copies = {}
 
     def send(self, slot, step, device, way=None):
-        start, rows = (0, 768) if way is None else (way * 384, 384)
-        place = self.w.at[(self.level + step) % 8 * 2 + self.core, pl.ds(start, rows)]
+        start, rows = (0, self.rows) if way is None else (way * self.rows // 2, self.rows // 2)
+        place = self.w.at[(self.level + step) % 8 * 2 + self.core, pl.ds(self.base + start, rows)]
         source = place if step else self.mine
         self.copies[slot] = remote(source, place, self.sends, self.recvs, slot, device)
 
@@ -234,44 +244,141 @@
             copy.wait_send()
 
 
+class Columns:
+    def __init__(self, mine, w_ref, parts, sends, recvs):
+        self.all = [
+            Column(mine.at[pl.ds(base, rows)], w_ref, base, rows, sends.at[i], recvs.at[i])
+            for i, (base, rows) in enumerate(parts)
+        ]
+        self.near = self.all[0].next + [self.all[0].other]
+
+    def start(self):
+        for column in self.all:
+            column.start()
+
+    def steps(self, *todo, then=None):
+        def run():
+            for which, t in todo:
+                self.all[which].step(t)
+            if then:
+                then()
+
+        return run
+
+    def finish(self):
+        for column in self.all:
+            column.finish()
+
+
 def normalized(values, gain):
     return values * lax.rsqrt(jnp.mean(values * values, axis=-1, keepdims=True) + 1e-06) * gain
 
 
-def pack_kernel(gate, up, down, w_query, w_key, w_value, w_out, attn_shard, moe_shard, down_shard):
-    key_cols = pl.ds(pl.multiple_of(lax.axis_index("expert") // 8 * HD, HD), HD)
-    attn_shard[0:256] = w_query[...]
-    attn_shard[256:512, 0:HD] = w_key[:, key_cols]
-    attn_shard[256:512, HD:] = w_value[:, key_cols]
-    attn_shard[512:768] = w_out[...]
-    for c in range(3):
-        cols = slice(c * 256, c * 256 + 256)
-        moe_shard[cols] = gate[:, cols]
-        moe_shard[FF + c * 256 : FF + c * 256 + 256] = up[:, cols]
-    for c in range(16):
-        down_shard[c * 48 : c * 48 + 48] = down[:, c * 256 : c * 256 + 256]
-
-
-def gather_kernel(
-    tokens, gain, routes, weights,
-    out, extra,
-    own, sends, recvs, local,
+class Share:
+    def __init__(self, spots, weights, wo, sends, recvs):
+        index = lax.axis_index("dp")
+        self.core = index % 2
+        self.other = {"dp": index + 1 - 2 * self.core}
+        self.spots, self.weights, self.wo, self.sends, self.recvs = spots, weights, wo, sends, recvs
+        self.copies = {}
+
+    def block(self, half, second, start, count):
+        return self.wo.at[half, pl.ds(4 * self.core + start, count), second]
+
+    def send(self, half, lane, source, target, device):
+        self.copies[half, lane] = remote(source, target, self.sends, self.recvs, half * 8 + lane, device)
+
+    def start(self):
+        for half, (f, s, device) in enumerate(self.spots):
+            source = self.weights.at[pl.ds(8 * half + 4 * self.core, 4), pl.ds(512, 256)]
+            for lane, step in ((0, 1), (1, 3)):
+                self.send(half, lane, source, self.block(half, s, 0, 4), device(f, turn(s, step)))
+
+    def forward(self):
+        for lane, step in ((0, 1), (1, 3)):
+            for half, (f, s, device) in enumerate(self.spots):
+                self.copies[half, lane].wait_recv()
+                here = self.block(half, turn(s, 4 - step), 2 * lane, 2)
+                self.send(half, 2 + lane, here, here, device(f, turn(s, step)))
+                here = self.block(half, turn(s, 4 - step), 0, 4)
+                self.send(half, 4 + lane, here, here, self.other)
+
+    def finish(self):
+        for lane in (0, 1):
+            for half, (f, s, device) in enumerate(self.spots):
+                self.copies[half, 2 + lane].wait_recv()
+                here = self.block(half, turn(s, 2), 2 * lane, 2)
+                self.send(half, 6 + lane, here, here, self.other)
+
+    def arrive(self):
+        for half in (0, 1):
+            for lane in range(4, 8):
+                self.copies[half, lane].wait_recv()
+
+    def drain(self):
+        for copy in self.copies.values():
+            copy.wait_send()
+
+
+def attend(
+    tokens, attn_gain, moe_gain, routes, route_weights, cosine, sine,
+    gate, up, down, w_query, w_key, w_value, w_out,
+    residual, everyone, w_late,
+    own, parts, wide, tall, shard, late_shard, x, w_all, wo, queries, keys, values, mixed, mx, moe_in, y, small, large,
+    in_sends, in_recvs, w_sends, w_recvs, wo_sends, wo_recvs, mx_sends, mx_recvs, sends, recvs, out_sends, out_recvs,
+    z_sends, z_recvs, local,
 ):
     spots = place()
     index = lax.axis_index("expert")
-    own[...] = normalized(tokens[...].astype(F32), gain[...]).astype(BF16)
-    keep = pltpu.make_async_copy(own, out.at[index], local)
-    keep.start()
-    meet(around(spots))
+    loads = [
+        pltpu.make_async_copy(source, target, local.at[i])
+        for i, (source, target) in enumerate(
+            (
+                (w_query, parts.at[0]),
+                (w_key, parts.at[1]),
+                (w_value, parts.at[2]),
+                (w_out, parts.at[3]),
+                (down, tall),
+                (gate, wide.at[0]),
+                (up, wide.at[1]),
+            )
+        )
+    ]
+    for copy in loads:
+        copy.start()
+    own[...] = normalized(tokens[...].astype(F32), attn_gain[...]).astype(BF16)
+    x[index] = own[...]
+    early = Columns(shard, w_all, EARLY, w_sends, w_recvs)
+    late = Columns(late_shard, w_late, LATE, z_sends, z_recvs)
+    share_out = Share(spots, w_all, wo, wo_sends, wo_recvs)
+    across = [device(f, turn(s, 2)) for f, s, device in spots]
+    meet(around(spots) + across + early.near)
 
     def block(r, half, second, start, rows):
         f, _, device = spots[half]
-        return out.at[device(turn(f, STEP[r]), second)["expert"], pl.ds(half * HALF + start, rows)]
-
-    gather = Gather(spots, block, sends, recvs, lambda half: own.at[pl.ds(half * HALF, HALF)], True)
+        return x.at[device(turn(f, STEP[r]), second)["expert"], pl.ds(half * HALF + start, rows)]
+
+    gather = Gather(spots, block, in_sends, in_recvs, lambda half: own.at[pl.ds(half * HALF, HALF)], True)
     gather.first_hop()
 
-    share = weights[...] / jnp.sum(weights[...], axis=0, keepdims=True)
+    for copy in loads:
+        copy.wait()
+    key_cols = pl.ds(pl.multiple_of(index // 8 * HD, HD), HD)
+    shard[0:256] = parts[0]
+    shard[256:512, 0:HD] = parts[1, :, key_cols]
+    shard[256:512, HD:] = parts[2, :, key_cols]
+    shard[512:768] = parts[3]
+    w_all[lax.axis_index("dp")] = shard[...]
+    early.start()
+    for c in range(6):
+        late_shard[c * 256 : c * 256 + 256] = wide[c // 3, :, c % 3 * 256 : c % 3 * 256 + 256]
+    for c in range(16):
+        late_shard[2 * FF + c * 48 : 2 * FF + c * 48 + 48] = tall[:, c * 256 : c * 256 + 256]
+
+    own_late = pltpu.make_async_copy(late_shard, w_late.at[lax.axis_index("dp")], local.at[7])
+    own_late.start()
+
+    share = route_weights[...] / jnp.sum(route_weights[...], axis=0, keepdims=True)
     high = share.astype(BF16).astype(F32)
     low = share - high
     at_row = lax.broadcasted_iota(jnp.int32, (EXTRA, TOK), 0)
@@ -280,99 +387,36 @@
         named = routes[k : k + 1]
         table += jnp.where(at_row == named, high[k : k + 1], 0.0)
         table += jnp.where(at_row == named + 16, low[k : k + 1], 0.0)
-    extra[...] = table.T.astype(BF16)
-
-    gather.rest()
-    keep.wait()
-
-
-class Share:
-    def __init__(self, spots, weights, wo, sends, recvs):
-        index = lax.axis_index("dp")
-        self.core = index % 2
-        self.other = {"dp": index + 1 - 2 * self.core}
-        self.spots, self.weights, self.wo, self.sends, self.recvs = spots, weights, wo, sends, recvs
-        self.copies = {}
-
-    def block(self, half, second, start, count):
-        return self.wo.at[half, pl.ds(4 * self.core + start, count), second]
-
-    def send(self, half, lane, source, target, device):
-        self.copies[half, lane] = remote(source, target, self.sends, self.recvs, half * 8 + lane, device)
-
-    def start(self):
-        for half, (f, s, device) in enumerate(self.spots):
-            source = self.weights.at[pl.ds(8 * half + 4 * self.core, 4), pl.ds(512, 256)]
-            for lane, step in ((0, 1), (1, 3)):
-                self.send(half, lane, source, self.block(half, s, 0, 4), device(f, turn(s, step)))
-
-    def forward(self):
-        for lane, step in ((0, 1), (1, 3)):
-            for half, (f, s, device) in enumerate(self.spots):
-                self.copies[half, lane].wait_recv()
-                here = self.block(half, turn(s, 4 - step), 2 * lane, 2)
-                self.send(half, 2 + lane, here, here, device(f, turn(s, step)))
-                here = self.block(half, turn(s, 4 - step), 0, 4)
-                self.send(half, 4 + lane, here, here, self.other)
-
-    def finish(self):
-        for lane in (0, 1):
-            for half, (f, s, device) in enumerate(self.spots):
-                self.copies[half, 2 + lane].wait_recv()
-                here = self.block(half, turn(s, 2), 2 * lane, 2)
-                self.send(half, 6 + lane, here, here, self.other)
-
-    def arrive(self):
-        for half in (0, 1):
-            for lane in range(4, 8):
-                self.copies[half, lane].wait_recv()
-
-    def drain(self):
-        for copy in self.copies.values():
-            copy.wait_send()
-
-
-def attend(
-    gathered, weights, tokens, cosine, sine, gain, extra, down_shard,
-    residual, everyone, down_all,
-    x, w, wo, queries, keys, values, mixed, mx, moe_in, y, small, large,
-    wo_sends, wo_recvs, mx_sends, mx_recvs, sends, recvs, out_sends, out_recvs, z_sends, z_recvs, local,
-):
-    spots = place()
-    load_w = pltpu.make_async_copy(weights.at[:, pl.ds(0, 512)], w, local.at[0])
-    load_w.start()
-    loads = []
-    for i in range(4):
-        loads.append(pltpu.make_async_copy(gathered.at[pl.ds(i * 4, 4)], x.at[pl.ds(i * 4, 4)], local.at[1 + i]))
-        loads[-1].start()
+    moe_in[:, D:] = table.T.astype(BF16)
+
+    gather.rest(
+        [
+            early.steps((0, 1)),
+            early.steps((1, 1), (0, 2)),
+            early.steps((1, 2)),
+            early.steps((0, 3), (1, 3), then=late.start),
+            early.steps((0, 4), (1, 4)),
+            late.steps((0, 1)),
+        ]
+    )
+    early.finish()
+    share_out.start()
+    owns = []
     for half, (f, s, _) in enumerate(spots):
-        loads.append(
-            pltpu.make_async_copy(
-                weights.at[pl.ds(8 * half, 8), pl.ds(512, 256)], wo.at[half, :, s], local.at[5 + half]
-            )
-        )
-        loads[-1].start()
-    share = Share(spots, weights, wo, wo_sends, wo_recvs)
-    across = [device(f, turn(s, 2)) for f, s, device in spots]
-    column = Column(down_shard, down_all, z_sends, z_recvs)
-    own_down = pltpu.make_async_copy(down_shard, down_all.at[lax.axis_index("dp")], local.at[7])
-    own_down.start()
-    meet(around(spots) + across + column.next + [column.other])
-    share.start()
-    column.start()
-    load_w.wait()
+        source = w_all.at[pl.ds(8 * half, 8), pl.ds(512, 256)]
+        owns.append(pltpu.make_async_copy(source, wo.at[half, :, s], local.at[5 + half]))
+        owns[-1].start()
 
     def rope(part, rows):
         return part * cosine[rows] + pltpu.roll(part, HD // 2, 1) * sine[rows]
 
     def project(i):
-        loads[i].wait()
         rows = slice(i * 256, i * 256 + 256)
         left = x[i * 4 : i * 4 + 4].reshape(256, D)
-        q = jnp.dot(left, w[:, 0:256].reshape(D, 256), preferred_element_type=F32)
+        q = jnp.dot(left, w_all[:, 0:256].reshape(D, 256), preferred_element_type=F32)
         for head in (0, 1):
             queries[head, rows] = rope(q[:, head * HD : (head + 1) * HD], rows).astype(BF16)
-        kv = jnp.dot(left, w[:, 256:512].reshape(D, 256), preferred_element_type=F32)
+        kv = jnp.dot(left, w_all[:, 256:512].reshape(D, 256), preferred_element_type=F32)
         keys[rows] = rope(kv[:, :HD], rows).astype(BF16)
         values[rows] = kv[:, HD:].astype(BF16)
 
@@ -392,8 +436,8 @@
 
     for i in range(4):
         project(i)
-    share.forward()
-    column.step(1)
+    share_out.forward()
+    late.steps((1, 1), (2, 1))()
     for i in range(4):
         attention(i)
 
@@ -413,12 +457,13 @@
         cols = pl.ds(pl.multiple_of(s * 256, 256), 256)
         keeps.append(pltpu.make_async_copy(rows_of(half, s), mx.at[half, :, :, cols], local.at[half]))
         keeps[-1].start()
-    share.finish()
-    for copy in keeps + loads[4:]:
+    share_out.finish()
+    late.steps((3, 1), (0, 2))()
+    for copy in keeps + owns:
         copy.wait()
     for copy in swaps:
         copy.wait_recv()
-    share.arrive()
+    share_out.arrive()
 
     fold = Fold(spots, y, small, large, None, sends, recvs, HALF)
     for half in (0, 1):
@@ -426,48 +471,46 @@
         for c in range(8):
             part = jnp.dot(left, wo[half, c].reshape(1024, 256), preferred_element_type=F32)
             y[half, :, :, c * 256 : c * 256 + 256] = part.astype(BF16).reshape(4, TOK, 256)
-
-    fold.start(0)
+        fold.start(0, (half,))
     for copy in swaps:
         copy.wait_send()
-    share.drain()
+    share_out.drain()
+    late.steps((1, 2), (2, 2))()
     fold.middle(0)
     for half in (0, 1):
         cols = slice(half * 2048, (half + 1) * 2048)
         residual[:, cols] = tokens[:, cols].astype(F32) + fold.total(half)
-    moe_in[:, 0:D] = normalized(residual[...], gain[...]).astype(BF16)
-    moe_in[:, D:] = extra[...]
-
-    def block(r, half, second, start, rows):
+    moe_in[:, 0:D] = normalized(residual[...], moe_gain[...]).astype(BF16)
+
+    def late_block(r, half, second, start, rows):
         return everyone.at[r, half, second, pl.ds(start, rows)]
 
-    gather = Gather(spots, block, out_sends, out_recvs, lambda half: moe_in.at[pl.ds(half * HALF, HALF)], False)
+    gather = Gather(spots, late_block, out_sends, out_recvs, lambda half: moe_in.at[pl.ds(half * HALF, HALF)], False)
     gather.first_hop()
     keeps = []
     for half, (_, s, _) in enumerate(spots):
-        keeps.append(pltpu.make_async_copy(gather.own(half), block(0, half, s, 0, HALF), local.at[half]))
+        keeps.append(pltpu.make_async_copy(gather.own(half), late_block(0, half, s, 0, HALF), local.at[half]))
         keeps[-1].start()
     fold.drain()
-    gather.second_hop()
-    gather.forward(0)
-    column.step(2)
-    gather.last_hop()
-    gather.forward(1)
-    gather.forward(2)
-    column.step(3)
-    gather.forward(3)
-    for r in range(4):
-        gather.finish(r)
-    column.step(4)
-    gather.drain()
+    late.steps((3, 2), (0, 3))()
+    gather.rest(
+        [
+            late.steps((1, 3)),
+            late.steps((2, 3)),
+            late.steps((3, 3), (0, 4)),
+            late.steps((1, 4), (2, 4)),
+            late.steps((3, 4)),
+            late.steps(),
+        ]
+    )
     for keep in keeps:
         keep.wait()
-    column.finish()
-    own_down.wait()
+    late.finish()
+    own_late.wait()
 
 
 def experts(
-    everyone, weights, down_all, residual,
+    everyone, weights, residual,
     out,
     g, w, wd, act, y, small, large, z, sends, recvs, load_g, load_w, load_down,
 ):
@@ -478,7 +521,7 @@
         part = (c // 2 + c % 2 * 3) * 256
         view = pl.ds(part, 256)
         feeds.append(pltpu.make_async_copy(weights.at[:, view], w.at[:, view], load_w.at[c]))
-    downs = pltpu.make_async_copy(down_all, wd, load_down)
+    downs = pltpu.make_async_copy(weights.at[:, pl.ds(2 * FF, FF)], wd, load_down)
     rows_of[3].start()
     for copy in feeds:
         copy.start()
@@ -520,15 +563,15 @@
     down(3)
     scatter.start(3)
     feed(2)
+    scatter.middle(3)
     down(2)
     scatter.start(2)
-    scatter.middle(3)
     feed(1)
-    down(1)
-    scatter.start(1)
     scatter.middle(2)
     scatter.finish(3)
     scatter.start(4)
+    down(1)
+    scatter.start(1)
     feed(0)
     scatter.middle(1)
     scatter.finish(2)
@@ -589,46 +632,25 @@
     route_weights,
 ):
     rows = tokens[0]
-    attn_shard, moe_shard, down_shard = pl.pallas_call(
-        pack_kernel,
-        out_shape=(
-            jax.ShapeDtypeStruct((768, 256), BF16),
-            jax.ShapeDtypeStruct((1536, 256), BF16),
-            jax.ShapeDtypeStruct((768, 256), BF16),
-        ),
-        in_specs=[VMEM] * 7,
-        out_specs=(VMEM, VMEM, VMEM),
-        compiler_params=pltpu.CompilerParams(vmem_limit_bytes=60 * MIB),
-        cost_estimate=cost(1 << 10, 4 * MIB),
-        name="pack_weights",
-    )(expert_gate[0], expert_up[0], expert_down[0], w_query, w_key, w_value, w_out)
-    attn_weights = lax.all_gather(attn_shard, "dp", axis=0)
-    moe_weights = lax.all_gather(moe_shard, "dp", axis=0)
-
-    gathered, extra = pl.pallas_call(
-        gather_kernel,
-        out_shape=(jax.ShapeDtypeStruct((16, TOK, D), BF16), jax.ShapeDtypeStruct((TOK, EXTRA), BF16)),
-        in_specs=[VMEM] * 4,
-        out_specs=(HBM, VMEM),
-        scratch_shapes=[pltpu.VMEM((TOK, D), BF16), SEMS, SEMS, pltpu.SemaphoreType.DMA],
-        compiler_params=params(0, 60),
-        cost_estimate=cost(1 << 10, MIB),
-        name="gather_tokens",
-    )(rows, attn_gain[None], routes[0].T, route_weights[0].T)
-
     cosine, sine = rope_tables()
-    residual, everyone, down_all = pl.pallas_call(
+    residual, everyone, w_late = pl.pallas_call(
         attend,
         out_shape=(
             jax.ShapeDtypeStruct((TOK, D), F32),
             jax.ShapeDtypeStruct((4, 2, 4, HALF, D + EXTRA), BF16),
-            jax.ShapeDtypeStruct((16, 768, 256), BF16),
+            jax.ShapeDtypeStruct((16, 2304, 256), BF16),
         ),
-        in_specs=[ANY, ANY, VMEM, VMEM, VMEM, VMEM, VMEM, ANY],
+        in_specs=[VMEM] * 7 + [ANY] * 7,
         out_specs=(VMEM, HBM, HBM),
         scratch_shapes=[
+            pltpu.VMEM((TOK, D), BF16),
+            pltpu.VMEM((4, 256, 256), BF16),
+            pltpu.VMEM((2, 256, FF), BF16),
+            pltpu.VMEM((48, D), BF16),
+            pltpu.VMEM((768, 256), BF16),
+            pltpu.VMEM((2304, 256), BF16),
             pltpu.VMEM((16, TOK, D), BF16),
-            pltpu.VMEM((16, 512, 256), BF16),
+            pltpu.VMEM((16, 768, 256), BF16),
             pltpu.VMEM((2, 8, 4, 256, 256), BF16),
             pltpu.VMEM((2, SEQ, HD), BF16),
             pltpu.VMEM((SEQ, HD), BF16),
@@ -639,6 +661,10 @@
             pltpu.VMEM((2, 4, TOK, 2048), BF16),
             pltpu.VMEM((2, 1, 2, HALF, 2048), BF16),
             pltpu.VMEM((2, 1, 2, TOK, 2048), BF16),
+            SEMS,
+            SEMS,
+            pltpu.SemaphoreType.DMA((2, 17)),
+            pltpu.SemaphoreType.DMA((2, 17)),
             pltpu.SemaphoreType.DMA((16,)),
             pltpu.SemaphoreType.DMA((16,)),
             pltpu.SemaphoreType.DMA((6,)),
@@ -647,19 +673,22 @@
             SEMS,
             SEMS,
             SEMS,
-            pltpu.SemaphoreType.DMA((17,)),
-            pltpu.SemaphoreType.DMA((17,)),
+            pltpu.SemaphoreType.DMA((4, 17)),
+            pltpu.SemaphoreType.DMA((4, 17)),
             pltpu.SemaphoreType.DMA((8,)),
         ],
-        compiler_params=params(1, 56),
-        cost_estimate=cost(1 << 10, MIB),
+        compiler_params=params(1, 60),
+        cost_estimate=cost(8 << 30, 64 * MIB),
         name="attention",
-    )(gathered, attn_weights, rows, cosine, sine, moe_gain[None], extra, down_shard)
+    )(
+        rows, attn_gain[None], moe_gain[None], routes[0].T, route_weights[0].T, cosine, sine,
+        expert_gate[0], expert_up[0], expert_down[0], w_query, w_key, w_value, w_out,
+    )
 
     layer_out = pl.pallas_call(
         experts,
         out_shape=jax.ShapeDtypeStruct((TOK, D), BF16),
-        in_specs=[ANY, ANY, ANY, VMEM],
+        in_specs=[ANY, ANY, VMEM],
         out_specs=VMEM,
         scratch_shapes=[
             pltpu.VMEM((4, 2, 4, HALF, D + EXTRA), BF16),
@@ -676,7 +705,7 @@
         compiler_params=params(2, 60),
         cost_estimate=cost(20 << 30, 200 * MIB),
         name="experts",
-    )(everyone, moe_weights, down_all, residual)
+    )(everyone, w_late, residual)
     return layer_out[None]
 
 

time: 230 us -> 209 us (0.909); the launches traced: 230 us -> 205 us
  between operations: 13.4 us -> 0.02 us
  Pallas kernels: 212 us -> 203 us
  waiting for transfers between devices: 2.99 us -> 0 us
    pallas_call x2 -> x0, Pallas kernels: 53.8 us -> none  [the longest x1 51.2 us: local(): pl.pallas_call(gather_kernel, out_shape=(jax.ShapeDtypeStruct((16, TOK, D...]
    pallas_call x1, Pallas kernels: 98.3 us -> 147 us  [local(): pl.pallas_call(attend, out_shape=(jax.ShapeDtypeStruct((TOK, D), F32), ja...]
    pallas_call x1, Pallas kernels: 59.5 us -> 56.4 us  [local(): pl.pallas_call(experts, out_shape=jax.ShapeDtypeStruct((TOK, D), BF16), i...]
  transfers between devices with their start and end apart: 2 -> 0, of which waited for: 1 -> 0; matrix products, arithmetic and copies ran while one was open for 0% -> 0% of each run, Pallas kernels for 65% -> 0%
where the time goes in v5:
time: 209 us; the launch traced here: 205 us
  Pallas kernels  203 us (97%)
    pallas_call x1, Pallas kernels, local(): pl.pallas_call(attend, out_shape=(jax.ShapeDtypeStruct((TOK, D), F32), ja...  147 us
    pallas_call x1, Pallas kernels, local(): pl.pallas_call(experts, out_shape=jax.ShapeDtypeStruct((TOK, D), BF16), i...  56.4 us

profile of v5, /device:TPU:1, one launch (start us, length us, event | category | flops | bytes accessed | tf_op | source)
XLA Modules:
  0.0 205.0 jit_solution(373238062529106952)
XLA Ops:
  0.0 146.7 %attention.1 = (f32[64,4096]{1,0:T(8,128)}, bf16[4,2,4,32,4224]{4,3,2,1,0:T(8,128)(2,1)}, bf16[16,2304,256]{2,1,0:T(8,128)(2,1)}) custom-call(bf16[64,4096]{1,0:T(8,128)(2,1)} %bitcast.14, f32[1,4096]{1,0:T(1,128)} %bitcast.18, f32[1,4096]{1,0:T(1,128)} %bitcast.19, s32[8,64]{1,0:T(8,128)} %bitcast.20, f32[8,64]{1,0:T(8,128)} %bitcast.21, ...), custom_call_target="tpu_custom_call" | custom-call | flops 8589934592 | bytes 67108864 | tf_op jit(solution)/shard_map/attention/pallas_call | solution.py:636
  146.7 56.4 %experts.1 = bf16[64,4096]{1,0:T(8,128)(2,1)} custom-call(bf16[4,2,4,32,4224]{4,3,2,1,0:T(8,128)(2,1)} %get-tuple-element.8.everyone, bf16[16,2304,256]{2,1,0:T(8,128)(2,1)} %get-tuple-element.9.weights, f32[64,4096]{1,0:T(8,128)} %get-tuple-element.10.residual), custom_call_target="tpu_custom_call" | custom-call | flops 21474836480 | bytes 209715200 | tf_op jit(solution)/shard_map/experts/pallas_call | solution.py:688
  203.1 1.9 copy.16

commit v6 on v5

--- a/solution.py
+++ b/solution.py
@@ -252,9 +252,9 @@
         ]
         self.near = self.all[0].next + [self.all[0].other]
 
-    def start(self):
-        for column in self.all:
-            column.start()
+    def start(self, parts=None):
+        for which in range(len(self.all)) if parts is None else parts:
+            self.all[which].start()
 
     def steps(self, *todo, then=None):
         def run():
@@ -389,24 +389,26 @@
         table += jnp.where(at_row == named + 16, low[k : k + 1], 0.0)
     moe_in[:, D:] = table.T.astype(BF16)
 
+    owns = []
+
+    def begin_share():
+        early.finish()
+        share_out.start()
+        for half, (f, s, _) in enumerate(spots):
+            source = w_all.at[pl.ds(8 * half, 8), pl.ds(512, 256)]
+            owns.append(pltpu.make_async_copy(source, wo.at[half, :, s], local.at[5 + half]))
+            owns[-1].start()
+
     gather.rest(
         [
             early.steps((0, 1)),
             early.steps((1, 1), (0, 2)),
-            early.steps((1, 2)),
-            early.steps((0, 3), (1, 3), then=late.start),
-            early.steps((0, 4), (1, 4)),
+            early.steps((1, 2), then=lambda: late.start((0,))),
+            early.steps((0, 3), (1, 3), then=lambda: late.start((1, 2, 3))),
+            early.steps((0, 4), (1, 4), then=begin_share),
             late.steps((0, 1)),
         ]
     )
-    early.finish()
-    share_out.start()
-    owns = []
-    for half, (f, s, _) in enumerate(spots):
-        source = w_all.at[pl.ds(8 * half, 8), pl.ds(512, 256)]
-        owns.append(pltpu.make_async_copy(source, wo.at[half, :, s], local.at[5 + half]))
-        owns[-1].start()
-
     def rope(part, rows):
         return part * cosine[rows] + pltpu.roll(part, HD // 2, 1) * sine[rows]
 

time: 209 us -> 210 us (level)
  no operation moved by 1% of the time
where the time goes in v6:
time: 210 us; the launch traced here: 206 us
  Pallas kernels  205 us (98%)
    pallas_call x1, Pallas kernels, local(): pl.pallas_call(attend, out_shape=(jax.ShapeDtypeStruct((TOK, D), F32), ja...  147 us
    pallas_call x1, Pallas kernels, local(): pl.pallas_call(experts, out_shape=jax.ShapeDtypeStruct((TOK, D), BF16), i...  58.1 us

profile of v6, /device:TPU:1, one launch (start us, length us, event | category | flops | bytes accessed | tf_op | source)
XLA Modules:
  0.0 206.5 jit_solution(3540521816331094426)
XLA Ops:
  0.0 146.5 %attention.1 = (f32[64,4096]{1,0:T(8,128)}, bf16[4,2,4,32,4224]{4,3,2,1,0:T(8,128)(2,1)}, bf16[16,2304,256]{2,1,0:T(8,128)(2,1)}) custom-call(bf16[64,4096]{1,0:T(8,128)(2,1)} %bitcast.14, f32[1,4096]{1,0:T(1,128)} %bitcast.18, f32[1,4096]{1,0:T(1,128)} %bitcast.19, s32[8,64]{1,0:T(8,128)} %bitcast.20, f32[8,64]{1,0:T(8,128)} %bitcast.21, ...), custom_call_target="tpu_custom_call" | custom-call | flops 8589934592 | bytes 67108864 | tf_op jit(solution)/shard_map/attention/pallas_call | solution.py:638
  146.5 58.1 %experts.1 = bf16[64,4096]{1,0:T(8,128)(2,1)} custom-call(bf16[4,2,4,32,4224]{4,3,2,1,0:T(8,128)(2,1)} %get-tuple-element.8.everyone, bf16[16,2304,256]{2,1,0:T(8,128)(2,1)} %get-tuple-element.9.weights, f32[64,4096]{1,0:T(8,128)} %get-tuple-element.10.residual), custom_call_target="tpu_custom_call" | custom-call | flops 21474836480 | bytes 209715200 | tf_op jit(solution)/shard_map/experts/pallas_call | solution.py:690
  204.6 1.9 copy.16
